TPU v7x, 256 devices: a whole 4x4x8 slice. The times are simulated.
256 devices in a mesh: seq: 32 (over x, z_hi, core), vocab: 8 (over z_lo, y).
Axes of the slice: x: 4, y: 4, z: 8 (z_hi: 4, z_lo: 2; z = z_hi * 2 + z_lo), core: 2. Of those that a mesh axis runs over, the one named last changes fastest.
Arguments:
- rollout_hidden: bfloat16 [1024, 4096], P('seq', 'vocab'), may hold values from -200 to 200
- trainer_hidden: bfloat16 [1024, 4096], P('seq'), may hold values from -200 to 200
- head_weight: bfloat16 [4096, 151552], P(None, ('seq', 'vocab')), may hold values from -1 to 1
- token_ids: int32 [1024], P('seq'), may hold values from 0 to 151551
- response_mask: int32 [1024], P('seq'), may hold values 0 or 1
- trainer_slot: int32 [1024], P('seq'), may hold values from 0 to 1023, as said below
Outputs:
- intersection: float32 [1024], P('seq')
- distance: float32 [1024], P('seq')
- import_weight: float32 [1024], P('seq')
Inputs may be any that keep to these rules, and one draw needn't show every extreme that they name: `trainer_slot`: a permutation of the 1024 trainer positions.
All inputs are finite; a program needn't handle non-finite values. No bound on the sum of `response_mask` on one device may be relied on, other than what follows from the above.
Results may differ from a plain program's by a relative error of at most 0.0025.
Values may be sent and summed in bfloat16 or wider, within the bound.
A program may use at most 128 MiB of HBM per device.

v0:
```python
import jax
import jax.numpy as jnp
from jax import lax
from jax.sharding import PartitionSpec as P


def per_device(rollout_hidden, trainer_hidden, head_weight, token_ids, response_mask, trainer_slot):
    row_count = trainer_slot.shape[0]
    total_rows = row_count * lax.axis_size("seq")
    column_count = head_weight.shape[1]
    whole_rows = lax.all_gather(rollout_hidden, "vocab", axis=1, tiled=True)
    roll_rows = lax.all_gather(whole_rows, "seq", axis=0, tiled=True)
    slots = lax.all_gather(trainer_slot, "seq", axis=0, tiled=True)
    train_rows = lax.all_gather(trainer_hidden, "seq", axis=0, tiled=True)
    sampled = lax.all_gather(token_ids, "seq", axis=0, tiled=True)
    roll_state = jnp.zeros((total_rows, column_count), jnp.float32)
    sampled_state = jnp.zeros((total_rows,), jnp.int32)
    roll_part = jnp.dot(roll_rows, head_weight, preferred_element_type=jnp.float32)
    train_part = jnp.dot(train_rows, head_weight, preferred_element_type=jnp.float32)
    roll_values, train_logit, sampled = (
        roll_state.at[slots].set(roll_part),
        train_part,
        lax.dynamic_update_slice_in_dim(sampled_state, sampled, jnp.int32(0), 0),
    )
    device_index = lax.axis_index("seq") * lax.axis_size("vocab") + lax.axis_index("vocab")
    offset = device_index * column_count
    matches = sampled[:, None] - offset == jnp.arange(column_count, dtype=jnp.int32)[None, :]
    pick_roll = jnp.sum(jnp.where(matches, roll_values, 0.0), axis=1)
    pick_train = jnp.sum(jnp.where(matches, train_logit, 0.0), axis=1)
    local_roll = jnp.max(roll_values, axis=1)
    local_train = jnp.max(train_logit, axis=1)
    top_roll, top_train = lax.pmax((local_roll, local_train), ("seq", "vocab"))
    total_roll, total_train, pick_roll, pick_train = lax.psum(
        (
            jnp.sum(jnp.exp(roll_values - top_roll[:, None]), axis=1),
            jnp.sum(jnp.exp(train_logit - top_train[:, None]), axis=1),
            pick_roll,
            pick_train,
        ),
        ("seq", "vocab"),
    )
    roll_prob = jnp.exp(roll_values - top_roll[:, None]) / total_roll[:, None]
    train_prob = jnp.exp(train_logit - top_train[:, None]) / total_train[:, None]
    shared, squares = lax.psum(
        (
            jnp.sum(jnp.minimum(roll_prob, train_prob), axis=1),
            jnp.sum((train_prob - roll_prob) ** 2, axis=1),
        ),
        ("seq", "vocab"),
    )
    log_ratio = (
        pick_train - top_train - jnp.log(total_train) - (pick_roll - top_roll - jnp.log(total_roll))
    )
    ratio = jnp.minimum(jnp.exp(log_ratio), 2.0)
    first_row = lax.axis_index("seq") * row_count
    shared = lax.dynamic_slice_in_dim(shared, first_row, row_count)
    squares = lax.dynamic_slice_in_dim(squares, first_row, row_count)
    ratio = lax.dynamic_slice_in_dim(ratio, first_row, row_count)
    mask_value = response_mask.astype(jnp.float32)
    return (shared * mask_value, jnp.sqrt(squares + 1e-06) * mask_value, ratio * mask_value)


def solution(mesh):
    placed = (
        P("seq", "vocab"),
        P("seq", None),
        P(None, ("seq", "vocab")),
        P("seq"),
        P("seq"),
        P("seq"),
    )
    return jax.shard_map(
        per_device,
        mesh=mesh,
        in_specs=placed,
        out_specs=(P("seq"), P("seq"), P("seq")),
        check_vma=False,
    )
```

profile of v0, /device:TPU:2, one launch (start us, length us, event | category | flops | bytes accessed | tf_op | source)
XLA Modules:
  0.0 445.4 jit_solution(1304798055220314257)
XLA Ops:
  7.2 0.0 all-gather.3.cloned.1.call-start
  7.2 31.6 %all_gather.16 = bf16[32,4096]{1,0:T(8,128)(2,1)} all-gather(bf16[32,512]{1,0:T(8,128)(2,1)} %param.6), channel_id=1, replica_groups=mesh['seq'=32,'vocab'=8] {'vocab'}, dimensions={1}, use_global_device_ids=true | all-gather | bytes 294912 | tf_op jit(solution)/shard_map/all_gather | solution.py:11
  38.8 0.0 all-gather.3.cloned.1.call-update
  38.8 0.0 all-gather.5.cloned.1.call-start
  38.9 0.7 all-gather.5.cloned.1.call-update
  39.6 1.3 dynamic-slice
  41.5 0.9 dynamic-update-slice
  42.4 0.8 dynamic-update-slice.1
  43.2 19.5 %all-reduce.2 = (s32[1024]{0:T(1024)S(1)}, s32[1024]{0:T(1024)S(1)}) all-reduce(s32[1024]{0:T(1024)S(1)} %dynamic-update-slice, s32[1024]{0:T(1024)S(1)} %dynamic-update-slice.1), channel_id=1, replica_groups=mesh['seq'=32,'vocab'=8] {'seq'}, use_global_device_ids=true, to_apply=%add | all-reduce | flops 2048 | bytes 16384
  62.7 56.1 %all-gather.3.cloned.1.call-done = bf16[1024,4096]{1,0:T(8,128)(2,1)} async-done(((bf16[32,4096]{1,0:T(8,128)(2,1)}), bf16[1024,4096]{1,0:T(8,128)(2,1)}) %all-gather.3.cloned.1.call-update) | async-done | bytes 8388624 | tf_op jit(solution)/shard_map/all_gather | solution.py:12
  118.8 11.6 %fusion.7 = f32[1024,592]{1,0:T(8,128)} fusion(bf16[1024,4096]{1,0:T(8,128)(2,1)} %all-gather.3.cloned.1.call-done, bf16[4096,592]{0,1:T(8,128)(2,1)} %param.8), kind=kOutput, calls=%fused_computation.21 | convolution fusion | flops 4966055936 | bytes 15663104 | tf_op jit(solution)/shard_map/dot_general | solution.py:18
  130.5 6.2 %scatter_custom_fusion = f32[1024,592]{1,0:T(8,128)S(1)} fusion(s32[1024]{0:T(1024)S(1)} %compare_select_fusion, f32[1024,592]{1,0:T(8,128)} %fusion.7, f32[]{:T(128)} %constant.12.clone.1), kind=kCustom, calls=%fused_computation.12 | custom fusion | bytes 2425344 | tf_op jit(solution)/shard_map/scatter | solution.py:21
  136.7 2.1 copy.11
  138.8 0.2 reduce_max.18
  139.0 59.5 %all-gather.5.cloned.1.call-done = bf16[1024,4096]{1,0:T(8,128)(2,1)} async-done(((bf16[32,4096]{1,0:T(8,128)(2,1)}), bf16[1024,4096]{1,0:T(8,128)(2,1)}) %all-gather.5.cloned.1.call-update) | async-done | bytes 8388624 | tf_op jit(solution)/shard_map/all_gather | solution.py:14
  198.5 10.6 %fusion.6 = (f32[1024]{0:T(1024)S(1)}, f32[1024,592]{0,1:T(8,128)}) fusion(bf16[1024,4096]{1,0:T(8,128)(2,1)} %all-gather.5.cloned.1.call-done, bf16[4096,592]{0,1:T(8,128)(2,1)} %param.8), kind=kOutput, calls=%fused_computation.20 | convolution fusion | flops 4966661120 | bytes 15667200 | tf_op jit(solution)/shard_map/dot_general | solution.py:19
  209.1 75.1 %all-reduce.5 = (f32[1024]{0:T(1024)S(1)}, f32[1024]{0:T(1024)S(1)}) all-reduce(f32[1024]{0:T(1024)S(1)} %get-tuple-element.20, f32[1024]{0:T(1024)S(1)} %reduce_max.18), channel_id=1, replica_groups=mesh['seq'=32,'vocab'=8] {'seq','vocab'}, use_global_device_ids=true, to_apply=%region_6.7 | all-reduce | flops 2048 | bytes 16384 | tf_op jit(solution)/shard_map/pmax | solution.py:32
  284.2 0.0 copy-done
  284.2 2.3 fusion.1
  286.5 74.2 %all-reduce.4 = (f32[1024]{0:T(1024)S(1)}, f32[1024]{0:T(1024)S(1)}) all-reduce(f32[1024]{0:T(1024)S(1)} %get-tuple-element.23, f32[1024]{0:T(1024)S(1)} %get-tuple-element.22), channel_id=1, replica_groups=mesh['seq'=32,'vocab'=8] {'seq','vocab'}, use_global_device_ids=true, to_apply=%region_8.9 | all-reduce | flops 2048 | bytes 16384 | tf_op jit(solution)/shard_map/psum | solution.py:33
  360.7 3.2 multiply_reduce_fusion
  363.9 74.1 %all-reduce.3 = (f32[1024]{0:T(1024)S(1)}, f32[1024]{0:T(1024)S(1)}, f32[1024]{0:T(1024)S(1)}, f32[1024]{0:T(1024)S(1)}) all-reduce(f32[1024]{0:T(1024)S(1)} %get-tuple-element.4, f32[1024]{0:T(1024)S(1)} %get-tuple-element.3, f32[1024]{0:T(1024)S(1)} %get-tuple-element.6, ...), channel_id=1, replica_groups=mesh['seq'=32,'vocab'=8] {'seq','vocab'}, use_global_device_ids=true, to_apply=%region_10.11 | all-reduce | flops 4096 | bytes 32768 | tf_op jit(solution)/shard_map/psum | solution.py:44
  438.0 0.0 copy-done.1
  438.0 0.6 dynamic-slice_multiply_fusion
  (7 shorter events, 0.0 us)
Async XLA Ops:
  7.2 111.6 %all-gather.3.cloned.1.call-start = ((), (), s32[]{:S(2)}) async-start(), calls=%async_computation | async-start | bytes 8650752 | tf_op jit(solution)/shard_map/all_gather | solution.py:12
  38.8 159.6 %all-gather.5.cloned.1.call-start = ((), (), s32[]{:S(2)}) async-start(), calls=%async_computation.1 | async-start | bytes 8650752 | tf_op jit(solution)/shard_map/all_gather | solution.py:14
  139.0 145.2 %copy-start = (f32[1024,592]{0,1:T(8,128)S(1)}, f32[1024,592]{0,1:T(8,128)}, u32[]{:S(2)}) copy-start(f32[1024,592]{0,1:T(8,128)} %copy.11) | copy-start | bytes 7274500
  360.7 77.3 %copy-start.1 = (s32[32]{0:T(128)S(1)}, s32[32]{0:T(128)}, u32[]{:S(2)}) copy-start(s32[32]{0:T(128)} %param.10) | copy-start | bytes 388
Sparse Core Ops, SparseCore 0:
  38.9 79.8 all-gather.2
  121.4 77.0 all-gather.4
where the time goes:
time: 447 us; the launch traced here: 445 us
  blocking collectives  274 us (61%)
  waiting for transfers between devices  116 us (26%)
  matrix products  22.3 us (5%)
  between operations  14.8 us (3%)
  local copies, waits for them, and re-layouts  11.3 us (3%)
  other arithmetic  6.4 us (1%)
    pmax x1, blocking collectives, per_device(): top_roll, top_train = lax.pmax((local_roll, local_train), ('seq', 'vocab'))  75.1 us
    psum x1, blocking collectives, per_device(): lax.psum((jnp.sum(jnp.exp(roll_values - top_roll[:, None]), axis=1), jnp....  74.2 us
    psum x1, blocking collectives, per_device(): lax.psum((jnp.sum(jnp.minimum(roll_prob, train_prob), axis=1), jnp.sum((t...  74.1 us
    all_gather x1, waiting for transfers between devices, per_device(): train_rows = lax.all_gather(trainer_hidden, 'seq', axis=0, tiled=True)  59.5 us
    all_gather x1, waiting for transfers between devices, per_device(): roll_rows = lax.all_gather(whole_rows, 'seq', axis=0, tiled=True)  56.1 us
    all_gather x1, blocking collectives, per_device(): whole_rows = lax.all_gather(rollout_hidden, 'vocab', axis=1, tiled=True)  31.6 us
    unnamed x1, blocking collectives  19.5 us
    dot_general x1, matrix products, per_device(): jnp.dot(roll_rows, head_weight, preferred_element_type=jnp.float32)  11.6 us
  transfers between devices with their start and end apart: 2, of which 2 were waited for; matrix products, arithmetic and copies ran while one was open for 5% of the time, Pallas kernels for 0%

commit v1 on v0

v1 whole, which is shorter than its diff:
```python
import jax
import jax.numpy as jnp
from jax import lax
from jax.experimental import pallas as pl
from jax.experimental.pallas import tpu as pltpu
from jax.sharding import PartitionSpec as P

MESH = pl.DeviceIdType.MESH
BF16 = jnp.bfloat16
F32 = jnp.float32
NX, NY, NZ, NH = 4, 4, 8, 4
ROWS = 32
HALF = 16
D = 4096
FEAT = 512
COLS = 592
TOK = 512
GROUP = 128


def kernel(roll_in, train_in, head_in, meta_in, mask_in, shared_out, dist_out, ratio_out,
           w, t, r, meta, onehot, perm, lt, lr, stat_r, stat_t, a1, a2, fin, out2, a3,
           ssem, in_sem, w_sem, tx, tz, r1z, m1z, r1x, m1x, msw, ry, rz, yr, zlate, sw, a_sem):
    s, v = lax.axis_index("seq"), lax.axis_index("vocab")
    x, zh, c = s // 8, (s // 2) % 4, s % 2
    zl, y = v // 4, v % 4
    z = zh * 2 + zl

    def dev(dx=0, dy=0, dz=0):
        xx, yy, zz = (x + dx + NX) % NX, (y + dy + NY) % NY, (z + dz + NZ) % NZ
        return ((xx * 4 + zz // 2) * 2 + c, (zz % 2) * 4 + yy)

    partner = (s + 1 - 2 * c, v)
    xm, xp, xo = (x + 3) % 4, (x + 1) % 4, (x + 2) % 4
    xg = (x, xm, xp, xo)
    zm, zp, zo = (zh + 3) % 4, (zh + 1) % 4, (zh + 2) % 4

    copies = [
        pltpu.make_async_copy(roll_in, r.at[v, c, x, :, zh], in_sem.at[0]),
        pltpu.make_async_copy(train_in, t.at[x, zh], in_sem.at[1]),
        pltpu.make_async_copy(meta_in, meta.at[c, x, zh], in_sem.at[2]),
        pltpu.make_async_copy(head_in, w.at[0], in_sem.at[3]),
    ]
    for cp in copies:
        cp.start()

    barrier = pltpu.get_barrier_semaphore()
    near = [partner] + [dev(dx=d) for d in (1, -1, 2)] + [dev(dy=d) for d in (1, -1)]
    near += [dev(dz=d) for d in (1, -1, 2, -2, 4)]
    for to in near:
        pl.semaphore_signal(barrier, inc=1, device_id=to, device_id_type=MESH)
    for cp in copies[:3]:
        cp.wait()
    pl.semaphore_wait(barrier, len(near))

    sends = []

    def put(src, dst, rsem, to):
        cp = pltpu.make_async_remote_copy(
            src_ref=src, dst_ref=dst, send_sem=ssem.at[len(sends)], recv_sem=rsem,
            device_id=to, device_id_type=MESH)
        cp.start()
        sends.append(cp)

    def same(ref, rsem, to):
        put(ref, ref, rsem, to)

    def got(ref, rsem):
        pltpu.make_async_remote_copy(
            src_ref=ref, dst_ref=ref, send_sem=rsem, recv_sem=rsem,
            device_id=partner, device_id_type=MESH).wait_recv()

    right, left = dev(dz=1), dev(dz=-1)
    xr, xl = dev(dx=1), dev(dx=-1)
    yu, yd = dev(dy=1), dev(dy=-1)

    own = r.at[v, c, x, :, zh]
    mine = meta.at[c, x, zh]
    for k, d in enumerate((2, -2, 4)):
        same(own, r1z.at[k], dev(dz=d))
    for k, d in enumerate((2, -2, 4)):
        same(mine, m1z.at[k], dev(dz=d))

    outward = dev(dz=2 * zl - 1)

    def ring_begin(g, xx):
        for k in range(2):
            h = zl * k + (1 - zl) * (1 - k)
            same(t.at[xx, zh, h], tz.at[g, 1 - zl, k], outward)

    inward = dev(dz=1 - 2 * zl)
    z_near, z_away = (1 - zl) * zm + zl * zp, (1 - zl) * zp + zl * zm

    def ring_block(xx, side, k):
        if side == 0:
            return t.at[xx, z_near if k < 2 else zo, (zl, 1 - zl, zl)[k]]
        return t.at[xx, z_away if k < 2 else zo, (1 - zl, zl, 1 - zl)[k]]

    def ring_step(g, xx, k, then=None):
        a, b = ring_block(xx, 0, k), ring_block(xx, 1, k)
        got(a, tz.at[g, zl, k])
        same(a, tz.at[g, zl, k], inward)
        if then is not None:
            then(a, 2 + 2 * k)
        got(b, tz.at[g, 1 - zl, k])
        if k == 0:
            same(b, tz.at[g, 1 - zl, 2], outward)
        if then is not None:
            then(b, 3 + 2 * k)

    def to_x(ref, n):
        same(ref, tx.at[0, n], xr)
        same(ref, tx.at[1, n], xl)

    ring_begin(0, x)
    to_x(t.at[x, zh, 0], 0)
    to_x(t.at[x, zh, 1], 1)
    copies[3].wait()
    put(w.at[0], w.at[1], w_sem, partner)

    v_z = (1 - zl) * 4 + y
    v_up, v_dn, v_far = zl * 4 + (y + 1) % 4, zl * 4 + (y + 3) % 4, zl * 4 + (y + 2) % 4
    w_up, w_dn, w_far = (1 - zl) * 4 + (y + 1) % 4, (1 - zl) * 4 + (y + 3) % 4, (1 - zl) * 4 + (y + 2) % 4

    def spread(g):
        block = r.at[v, c, xg[g]]
        same(block, ry.at[0, 0, g], yu)
        same(block, ry.at[1, 0, g], yd)
        same(r.at[v, c, xg[g], 0], rz.at[0, g], right)
        same(r.at[v, c, xg[g], 1], rz.at[1, g], left)

    def swap(n, vv):
        same(r.at[vv, c], sw.at[n], partner)

    def swapped(n, vv):
        got(r.at[vv, 1 - c], sw.at[n])

    for k, zz in enumerate((zm, zp, zo)):
        got(r.at[v, c, x, :, zz], r1z.at[k])
    same(r.at[v, c, x], r1x.at[0, 0], xr)
    same(r.at[v, c, x], r1x.at[1, 0], xl)
    spread(0)
    for k, zz in enumerate((zm, zp, zo)):
        got(meta.at[c, x, zz], m1z.at[k])
    for k, d in enumerate((1, -1, 2)):
        same(meta.at[c, x], m1x.at[k], dev(dx=d))
    got(t.at[xm, zh, 0], tx.at[0, 0])
    same(t.at[xm, zh, 0], tx.at[0, 8], xr)
    got(t.at[xp, zh, 0], tx.at[1, 0])
    got(t.at[xp, zh, 1], tx.at[1, 1])
    same(t.at[xp, zh, 1], tx.at[1, 8], xl)
    got(t.at[xm, zh, 1], tx.at[0, 1])
    ring_step(0, x, 0, to_x)
    got(r.at[v, c, xm], r1x.at[0, 0])
    same(r.at[v, c, xm, 0], r1x.at[0, 1], xr)
    spread(1)
    got(r.at[v, c, xp], r1x.at[1, 0])
    same(r.at[v, c, xp, 1], r1x.at[1, 1], xl)
    spread(2)
    ring_step(0, x, 1, to_x)

    def cross(g):
        got(r.at[v_z, c, xg[g], 0], rz.at[0, g])
        got(r.at[v_z, c, xg[g], 1], rz.at[1, g])
        same(r.at[v_z, c, xg[g]], ry.at[0, 1, g], yu)
        same(r.at[v_z, c, xg[g]], ry.at[1, 1, g], yd)

    def relay(g):
        got(r.at[v_up, c, xg[g]], ry.at[1, 0, g])
        same(r.at[v_up, c, xg[g], 0], yr.at[1, g], yd)
        got(r.at[v_dn, c, xg[g]], ry.at[0, 0, g])
        same(r.at[v_dn, c, xg[g], 1], yr.at[0, g], yu)

    got(r.at[v, c, xo, 0], r1x.at[0, 1])
    got(r.at[v, c, xo, 1], r1x.at[1, 1])
    spread(3)
    swap(0, v)
    for k, xx in enumerate((xm, xp, xo)):
        got(meta.at[c, xx], m1x.at[k])
    same(meta.at[c], msw, partner)
    got(t.at[xo, zh, 0], tx.at[0, 8])
    got(t.at[xo, zh, 1], tx.at[1, 8])
    ring_begin(1, xo)
    cross(0)
    relay(0)
    ring_step(0, x, 2, to_x)
    cross(1)
    cross(2)
    relay(1)
    relay(2)

    got(meta.at[1 - c], msw)
    place = lax.broadcasted_iota(jnp.int32, (TOK, GROUP), 0)
    for cc in range(2):
        for xx in range(NX):
            slot = meta[cc, xx, 0, 0:1, :]
            for zz in range(1, NH):
                slot = slot + meta[cc, xx, zz, 0:1, :]
            token = (slot >> 6) * ROWS + (slot & (ROWS - 1))
            token = jnp.where(((slot >> 5) & 1) == c, token, -1)
            n = cc * NX + xx
            onehot[:, n * GROUP:(n + 1) * GROUP] = jnp.where(place == token, 1.0, 0.0).astype(BF16)

    def rollout_part(vv, first):
        rows = r[vv].reshape(2 * TOK, FEAT)
        perm[...] = jnp.dot(onehot[...], rows, preferred_element_type=F32).astype(BF16)
        for n in range(2):
            part = jnp.dot(perm[...], w[n, pl.ds(pl.multiple_of(vv * FEAT, FEAT), FEAT), :], preferred_element_type=F32)
            if first:
                lr[n] = part
            else:
                lr[n] += part

    def trainer_part(xa, xb):
        def step(k, carry):
            f = pl.ds(pl.multiple_of(k * FEAT, FEAT), FEAT)
            a = t[xa, :, :, :, f].reshape(GROUP, FEAT)
            b = t[xb, :, :, :, f].reshape(GROUP, FEAT)
            rows = jnp.concatenate([a, b], axis=0)
            keep = jnp.where(k == 0, 0.0, 1.0)
            for n in range(2):
                part = jnp.dot(rows, w[n, f, :], preferred_element_type=F32)

                @pl.when(k == 0)
                def _():
                    lt[n, xa] = part[:GROUP]
                    lt[n, xb] = part[GROUP:]

                @pl.when(k > 0)
                def _():
                    lt[n, xa] += part[:GROUP]
                    lt[n, xb] += part[GROUP:]
            return carry
        lax.fori_loop(0, D // FEAT, step, 0)

    lane = lax.broadcasted_iota(jnp.int32, (GROUP, 128), 1)
    column = lax.broadcasted_iota(jnp.int32, (GROUP, COLS), 1)
    offsets = ((s * 8 + v) * COLS, ((s + 1 - 2 * c) * 8 + v) * COLS)
    diagonal = lax.broadcasted_iota(jnp.int32, (GROUP, 128), 0) == lane

    def local_stats(logit, stat, xx, rows):
        ids = meta[c, xx, 0, 1:2, :]
        for zz in range(1, NH):
            ids = ids + meta[c, xx, zz, 1:2, :]
        ids = jnp.sum(jnp.where(diagonal, ids, 0), axis=1, keepdims=True)
        parts = [logit[(n,) + rows] for n in range(2)]
        top = jnp.maximum(jnp.max(parts[0], axis=1, keepdims=True), jnp.max(parts[1], axis=1, keepdims=True))
        total = jnp.zeros((GROUP, 1), F32)
        pick = jnp.zeros((GROUP, 1), F32)
        for n in range(2):
            e = jnp.exp(parts[n] - top)
            logit[(n,) + rows] = e
            total = total + jnp.sum(e, axis=1, keepdims=True)
            pick = pick + jnp.sum(jnp.where(column == ids - offsets[n], parts[n], 0.0), axis=1, keepdims=True)
        table = jnp.where(lane == 0, top, jnp.where(lane == 1, total, jnp.where(lane == 2, pick, 0.0)))
        stat[xx] = jnp.transpose(table)[:8]

    got(w.at[1], w_sem)
    swapped(0, v)
    rollout_part(v, True)

    cross(3)
    relay(3)
    swap(1, v_z)
    swap(2, v_up)
    swap(3, v_dn)
    ring_step(1, xo, 0)

    def far(g):
        got(r.at[v_far, c, xg[g], 0], yr.at[1, g])
        same(r.at[v_far, c, xg[g], 0], zlate.at[0, g], right)
        got(r.at[v_far, c, xg[g], 1], yr.at[0, g])
        same(r.at[v_far, c, xg[g], 1], zlate.at[1, g], left)

    far(0)
    far(1)
    ring_step(1, xo, 1)
    swapped(1, v_z)
    rollout_part(v_z, False)
    far(2)
    far(3)
    swap(4, v_far)
    ring_step(1, xo, 2)
    swapped(2, v_up)
    rollout_part(v_up, False)
    swapped(3, v_dn)
    rollout_part(v_dn, False)
    trainer_part(x, xo)
    for n in range(2, 8):
        side = (n - 2) % 2
        k = (n - 2) // 2
        got(ring_block(xm, side, k), tx.at[0, n])
        got(ring_block(xp, side, k), tx.at[1, n])
    trainer_part(xm, xp)

    def train_stats(xx, carry):
        local_stats(lt, stat_t, xx, (xx,))
        return carry
    lax.fori_loop(0, NX, train_stats, 0)

    swapped(4, v_far)
    rollout_part(v_far, False)
    for g in range(4):
        got(r.at[w_up, c, xg[g]], ry.at[1, 1, g])
        got(r.at[w_dn, c, xg[g]], ry.at[0, 1, g])
    swap(5, w_up)
    swap(6, w_dn)
    for g in range(4):
        got(r.at[w_far, c, xg[g], 0], zlate.at[0, g])
        got(r.at[w_far, c, xg[g], 1], zlate.at[1, g])
    swap(7, w_far)
    swapped(5, w_up)
    rollout_part(w_up, False)
    swapped(6, w_dn)
    rollout_part(w_dn, False)
    swapped(7, w_far)
    rollout_part(w_far, False)

    def roll_stats(xx, carry):
        local_stats(lr, stat_r, xx, (pl.ds(pl.multiple_of(xx * GROUP, GROUP), GROUP),))
        return carry
    lax.fori_loop(0, NX, roll_stats, 0)

    for n in range(2):
        a1[0, 0, n] = stat_r[:, n, :]
        a1[0, 1, n] = stat_t[:, n, :]

    def exchange(buf, count, sem, to):
        def start(d, carry):
            pltpu.make_async_remote_copy(
                src_ref=buf.at[0], dst_ref=buf.at[d], send_sem=a_sem.at[sem], recv_sem=a_sem.at[sem + 1],
                device_id=to(d), device_id_type=MESH).start()
            return carry
        lax.fori_loop(1, count, start, 0)
        rest = buf.at[pl.ds(1, count - 1)]
        done = pltpu.make_async_remote_copy(
            src_ref=rest, dst_ref=rest, send_sem=a_sem.at[sem], recv_sem=a_sem.at[sem + 1],
            device_id=partner, device_id_type=MESH)
        done.wait_recv()
        return done

    def merge(buf, count):
        top = buf[0, :, 0]
        for d in range(1, count):
            top = jnp.maximum(top, buf[d, :, 0])
        total = jnp.zeros_like(top)
        for d in range(count):
            total = total + buf[d, :, 1] * jnp.exp(buf[d, :, 0] - top)
        return top, total

    done1 = exchange(a1, 16, 0, lambda d: dev(dx=d // 4, dy=d % 4))
    top, total = merge(a1, 16)
    a2[0, :, 0] = top
    a2[0, :, 1] = total
    done2 = exchange(a2, 8, 2, lambda d: dev(dz=d))
    top, total = merge(a2, 8)
    fin[:, 0] = top
    fin[:, 1] = total

    def compare(xx, carry):
        rows = pl.ds(pl.multiple_of(xx * GROUP, GROUP), GROUP)
        scale_r = jnp.exp(stat_r[xx, 0:1, :] - fin[0, 0, pl.ds(xx, 1), :]) / fin[0, 1, pl.ds(xx, 1), :]
        scale_t = jnp.exp(stat_t[xx, 0:1, :] - fin[1, 0, pl.ds(xx, 1), :]) / fin[1, 1, pl.ds(xx, 1), :]
        scale_r = jnp.sum(jnp.where(diagonal, scale_r, 0.0), axis=1, keepdims=True)
        scale_t = jnp.sum(jnp.where(diagonal, scale_t, 0.0), axis=1, keepdims=True)
        shared = jnp.zeros((GROUP, 1), F32)
        squares = jnp.zeros((GROUP, 1), F32)
        for n in range(2):
            p = lr[n, rows] * scale_r
            q = lt[n, xx] * scale_t
            shared = shared + jnp.sum(jnp.minimum(p, q), axis=1, keepdims=True)
            squares = squares + jnp.sum((q - p) * (q - p), axis=1, keepdims=True)
        table = jnp.where(lane == 0, shared, jnp.where(lane == 1, squares, 0.0))
        table = jnp.transpose(table)[:2]
        values = (table[0:1], table[1:2], stat_r[xx, 2:3, :], stat_t[xx, 2:3, :])
        part = lax.broadcasted_iota(jnp.int32, (1, 128), 1) // ROWS
        for zz in range(NH):
            line = jnp.zeros((1, 128), F32)
            for k in range(4):
                line = line + jnp.where(part == k, pltpu.roll(values[k], ((k - zz) % 4) * ROWS, 1), 0.0)
            out2[xx, zz] = line
        return carry
    lax.fori_loop(0, NX, compare, 0)

    a3[0] = out2[x, zh]

    def send(d, carry):
        dx, dy, dz = d // 32, (d // 8) % 4, d % 8
        pltpu.make_async_remote_copy(
            src_ref=out2.at[(x + dx) % NX, ((z + dz) % NZ) // 2], dst_ref=a3.at[d],
            send_sem=a_sem.at[4], recv_sem=a_sem.at[5], device_id=dev(dx, dy, dz), device_id_type=MESH).start()
        return carry
    lax.fori_loop(1, 128, send, 0)
    rest = a3.at[pl.ds(1, 127)]
    done3 = pltpu.make_async_remote_copy(
        src_ref=rest, dst_ref=rest, send_sem=a_sem.at[4], recv_sem=a_sem.at[5],
        device_id=partner, device_id_type=MESH)
    for cp in sends:
        cp.wait_send()
    done1.wait_send()
    done2.wait_send()
    done3.wait_recv()
    sums = jnp.sum(a3[...], axis=0)
    shift = (NH - zh) % NH * ROWS
    own_top = [pltpu.roll(fin[n, 0, pl.ds(x, 1), :], shift, 1)[:, :ROWS] for n in range(2)]
    own_total = [pltpu.roll(fin[n, 1, pl.ds(x, 1), :], shift, 1)[:, :ROWS] for n in range(2)]
    mask = mask_in[...].astype(F32)
    pick_r = pltpu.roll(sums, 2 * ROWS, 1)[:, :ROWS]
    pick_t = pltpu.roll(sums, ROWS, 1)[:, :ROWS]
    squares = pltpu.roll(sums, 3 * ROWS, 1)[:, :ROWS]
    log_ratio = pick_t - own_top[1] - jnp.log(own_total[1]) - (pick_r - own_top[0] - jnp.log(own_total[0]))
    shared_out[...] = sums[:, :ROWS] * mask
    dist_out[...] = jnp.sqrt(squares + 1e-06) * mask
    ratio_out[...] = jnp.minimum(jnp.exp(log_ratio), 2.0) * mask
    done3.wait_send()


def per_device(rollout_hidden, trainer_hidden, head_weight, token_ids, response_mask, trainer_slot):
    zh = (lax.axis_index("seq") // 2) % 4
    here = jnp.arange(NH, dtype=jnp.int32) == zh
    slots = jnp.where(here[None, :, None], trainer_slot.reshape(2, 1, HALF), 0).reshape(1, 128)
    ids = jnp.where(here[:, None], token_ids.reshape(1, ROWS), 0).reshape(1, 128)
    meta = jnp.concatenate([slots, ids], axis=0)
    dma, reg = pltpu.SemaphoreType.DMA, pl.BlockSpec(memory_space=pl.ANY)
    vmem = pl.BlockSpec(memory_space=pltpu.VMEM)
    outs = pl.pallas_call(
        kernel,
        out_shape=[jax.ShapeDtypeStruct((1, ROWS), F32)] * 3,
        in_specs=[reg, reg, reg, reg, vmem],
        out_specs=[vmem] * 3,
        scratch_shapes=[
            pltpu.VMEM((2, D, COLS), BF16),
            pltpu.VMEM((NX, NH, 2, HALF, D), BF16),
            pltpu.VMEM((8, 2, NX, 2, NH, HALF, FEAT), BF16),
            pltpu.VMEM((2, NX, NH, 2, 128), jnp.int32),
            pltpu.VMEM((TOK, 2 * TOK), BF16),
            pltpu.VMEM((TOK, FEAT), BF16),
            pltpu.VMEM((2, NX, GROUP, COLS), F32),
            pltpu.VMEM((2, TOK, COLS), F32),
            pltpu.VMEM((NX, 8, 128), F32),
            pltpu.VMEM((NX, 8, 128), F32),
            pltpu.VMEM((16, 2, 2, NX, 128), F32),
            pltpu.VMEM((8, 2, 2, NX, 128), F32),
            pltpu.VMEM((2, 2, NX, 128), F32),
            pltpu.VMEM((NX, NH, 1, 128), F32),
            pltpu.VMEM((128, 1, 128), F32),
            dma((128,)), dma((4,)), dma,
            dma((2, 9)), dma((2, 2, 3)), dma((3,)), dma((3,)), dma((2, 2)), dma((3,)), dma,
            dma((2, 2, 4)), dma((2, 4)), dma((2, 4)), dma((2, 4)), dma((8,)), dma((6,)),
        ],
        compiler_params=pltpu.CompilerParams(
            collective_id=0, has_side_effects=True, vmem_limit_bytes=60 * 1024 * 1024),
        cost_estimate=pl.CostEstimate(
            flops=2 * 2 * TOK * D * 2 * COLS + 2 * TOK * 2 * TOK * D, bytes_accessed=D * COLS * 2, transcendentals=2 * TOK * 2 * COLS),
    )(rollout_hidden.reshape(2, HALF, FEAT), trainer_hidden.reshape(2, HALF, D), head_weight, meta,
      response_mask.reshape(1, ROWS))
    return tuple(o.reshape(ROWS) for o in outs)


def solution(mesh):
    placed = (
        P("seq", "vocab"),
        P("seq", None),
        P(None, ("seq", "vocab")),
        P("seq"),
        P("seq"),
        P("seq"),
    )
    return jax.shard_map(
        per_device,
        mesh=mesh,
        in_specs=placed,
        out_specs=(P("seq"), P("seq"), P("seq")),
        check_vma=False,
    )
```

time: 447 us -> 129 us (0.29)
  blocking collectives: 274 us -> 0 us
  waiting for transfers between devices: 116 us -> 0 us
  Pallas kernels: 0 us -> 114 us
  matrix products: 22.3 us -> 0 us
  between operations: 14.8 us -> 0.68 us
  other arithmetic: 6.4 us -> 1.39 us
    psum x2 -> x0, blocking collectives: 148 us -> none  [the longest x1 74.2 us: per_device(): lax.psum((jnp.sum(jnp.exp(roll_values - top_roll[:, None]), axis=1), jnp....]
    all_gather x2 -> x0, waiting for transfers between devices: 116 us -> none  [the longest x1 59.5 us: per_device(): train_rows = lax.all_gather(trainer_hidden, 'seq', axis=0, tiled=True)]
    pallas_call x0 -> x1, Pallas kernels: none -> 114 us  [per_device(): pl.pallas_call(kernel, out_shape=[jax.ShapeDtypeStruct((1, ROWS), F32)] *...]
    pmax x1 -> x0, blocking collectives: 75.1 us -> none  [per_device(): top_roll, top_train = lax.pmax((local_roll, local_train), ('seq', 'vocab'))]
    all_gather x1 -> x0, blocking collectives: 31.6 us -> none  [per_device(): whole_rows = lax.all_gather(rollout_hidden, 'vocab', axis=1, tiled=True)]
    dot_general x2 -> x0, matrix products: 22.3 us -> none  [the longest x1 11.6 us: per_device(): jnp.dot(roll_rows, head_weight, preferred_element_type=jnp.float32)]
    unnamed x1 -> x0, blocking collectives: 19.5 us -> none
    scatter x2 -> x0, local copies, waits for them, and re-layouts: 8.3 us -> none  [per_device(): roll_state.at[slots].set(roll_part)]
  transfers between devices with their start and end apart: 2 -> 0, of which waited for: 2 -> 0; matrix products, arithmetic and copies ran while one was open for 5% -> 0% of each run, Pallas kernels for 0% -> 0%
where the time goes in v1:
time: 129 us; the launch traced here: 128 us
  Pallas kernels  114 us (88%)
  local copies, waits for them, and re-layouts  12.1 us (9%)
  other arithmetic  1.39 us (1%)
    pallas_call x1, Pallas kernels, per_device(): pl.pallas_call(kernel, out_shape=[jax.ShapeDtypeStruct((1, ROWS), F32)] *...  114 us
    unnamed x4, local copies, waits for them, and re-layouts  11.2 us

profile of v1, /device:TPU:2, one launch (start us, length us, event | category | flops | bytes accessed | tf_op | source)
XLA Modules:
  0.0 128.2 jit_solution(4940358435009677246)
XLA Ops:
  0.7 0.7 broadcast_in_dim.45
  1.4 0.7 broadcast_select_fusion.1
  2.1 0.1 select_n.44
  2.2 0.1 broadcast_select_fusion
  2.3 0.1 select_n.42
  2.4 0.6 pad_add_fusion.meta_in
  3.0 7.7 %copy.9.head_in = bf16[4096,592]{1,0:T(8,128)(2,1)} copy(bf16[4096,592]{0,1:T(8,128)(2,1)} %param.8) | data formatting | bytes 9699328 | tf_op args[2]
  10.7 114.1 %shard_map.85 = (f32[1,32]{1,0:T(1,128)}, f32[1,32]{1,0:T(1,128)}, f32[1,32]{1,0:T(1,128)}) custom-call(bf16[2,16,512]{2,1,0:T(8,128)(2,1)} %bitcast.7, bf16[2,16,4096]{2,1,0:T(8,128)(2,1)} %bitcast.6, bf16[4096,592]{1,0:T(8,128)(2,1)} %copy.9.head_in, s32[2,128]{1,0:T(2,128)} %pad_add_fusion.meta_in, s32[1,32]{1,0:T(1,128)} %bitcast.8), custom_call_target="tpu_custom_call" | custom-call | flops 14227079168 | bytes 4849664 | tf_op jit(solution)/shard_map/pallas_call | solution.py:426
  124.8 1.2 copy.13
  126.0 1.1 copy.14
  127.1 1.1 copy.15
  (1 shorter events, 0.0 us)

commit v2 on v0

v2 whole, which is shorter than its diff:
```python
import jax
import jax.numpy as jnp
from jax import lax
from jax.experimental import pallas as pl
from jax.experimental.pallas import tpu as pltpu
from jax.sharding import PartitionSpec as P

MESH = pl.DeviceIdType.MESH
BF16 = jnp.bfloat16
F32 = jnp.float32
NX, NY, NZ, NH = 4, 4, 8, 4
ROWS = 32
HALF = 16
D = 4096
FEAT = 512
COLS = 592
TOK = 512
GROUP = 128
PART = 1024
ARRIVALS = 86

ORDER = (
    ("start", 0), ("fx", 1), ("tzown", 1), ("fx", 3), ("tzown", 0), ("sx", 0),
    ("sx", 1), ("fx", 0), ("head", 0), ("tzown", 3), ("sx", 2), ("sz", 1),
    ("tl", 1), ("tr", 1), ("tzown", 2), ("near0", 1), ("sz", 0), ("spread", 0),
    ("meta1", 0), ("sz", 2), ("tr", 0), ("tl", 0), ("near0", 0), ("s2r", 1),
    ("s2l", 1), ("near0", 3), ("fx", 10), ("own1", 1), ("own1", 3), ("relayu", 0),
    ("relayd", 0), ("near0", 2), ("fx", 8), ("meta2", 0), ("away0", 1), ("cross", 0),
    ("fx", 4), ("own1", 2), ("near1", 1), ("onehot", 0), ("s2l", 0), ("fx", 5),
    ("own1", 0), ("s3", 1), ("near1", 3), ("s2r", 0), ("fx", 6), ("away0", 0),
    ("near0", 5), ("s2r", 2), ("s2l", 2), ("spread", 2), ("fx", 9), ("near1", 2),
    ("away1", 1), ("fx", 14), ("s3", 0), ("near1", 0), ("fx", 2), ("relayu", 2),
    ("relayd", 2), ("swap", 0), ("s3", 2), ("spread", 3), ("relayu", 1), ("relayd", 1),
    ("fx", 12), ("spread", 1), ("cross", 2), ("fx", 15), ("R", 0), ("near0", 4),
    ("away1", 0), ("fx", 7), ("swap", 2), ("swap", 3), ("T", 2), ("far", 1),
    ("relayd", 3), ("relayu", 3), ("fx", 11), ("near1", 5), ("R", 2), ("near1", 4),
    ("swap", 1), ("cross", 1), ("R", 3), ("far", 2), ("fx", 13), ("cross", 3),
    ("swap", 4), ("T", 3), ("far", 3), ("R", 1), ("far", 0), ("T", 1),
    ("R", 4), ("swap", 5), ("swap", 6), ("T", 0), ("TS", 0), ("swap", 7),
    ("R", 5), ("R", 6), ("R", 7), ("RS", 0),
)


def kernel(roll_in, train_in, head_in, slot_in, ids_in, out,
           w, t, r, slot_v, ids_v, line, meta, onehot, perm, lt, lr, stat_r, stat_t, a1, a2, fin, out2, a3,
           ssem, rsem, in_sem, a_sem):
    s, v = lax.axis_index("seq"), lax.axis_index("vocab")
    x, zh, c = s // 8, (s // 2) % 4, s % 2
    zl, y = v // 4, v % 4
    z = zh * 2 + zl

    def dev(dx=0, dy=0, dz=0):
        xx, yy, zz = (x + dx + NX) % NX, (y + dy + NY) % NY, (z + dz + NZ) % NZ
        return ((xx * 4 + zz // 2) * 2 + c, (zz % 2) * 4 + yy)

    partner = (s + 1 - 2 * c, v)
    xm, xp, xo = (x + 3) % 4, (x + 1) % 4, (x + 2) % 4
    xg = (x, xm, xp, xo)
    zm, zp, zo = (zh + 3) % 4, (zh + 1) % 4, (zh + 2) % 4

    barrier = pltpu.get_barrier_semaphore()
    near = [dev(dz=d) for d in (4, 2, -2)] + [dev(dx=2)] + [dev(dx=d) for d in (1, -1)]
    near += [dev(dy=d) for d in (1, -1)] + [dev(dz=d) for d in (1, -1)] + [partner]
    for to in near:
        pl.semaphore_signal(barrier, inc=1, device_id=to, device_id_type=MESH)

    copies = [
        pltpu.make_async_copy(slot_in, slot_v, in_sem.at[6]),
        pltpu.make_async_copy(ids_in, ids_v, in_sem.at[7]),
        pltpu.make_async_copy(roll_in, r.at[v, c, x, :, zh], in_sem.at[0]),
    ]
    for q in range(4):
        copies.append(pltpu.make_async_copy(train_in.at[:, q * PART:(q + 1) * PART], t.at[x, zh, q], in_sem.at[1 + q]))
    copies.append(pltpu.make_async_copy(head_in, w.at[:COLS], in_sem.at[5]))
    for cp in copies:
        cp.start()
    for cp in copies[:2]:
        cp.wait()
    lanes = lax.broadcasted_iota(jnp.int32, (1, 128), 1)
    line[0:1, :ROWS] = slot_v[...]
    line[1:2, :ROWS] = ids_v[...]
    slots, ids = line[0:1, :], line[1:2, :]
    low = jnp.where(lanes // HALF == zh, pltpu.roll(slots, zh * HALF, 1), 0)
    high = jnp.where(lanes // HALF == NH + zh, pltpu.roll(slots, (NH - 1 + zh) * HALF, 1), 0)
    meta[c, x, zh, 0:1, :] = low + high
    meta[c, x, zh, 1:2, :] = jnp.where(lanes // ROWS == zh, pltpu.roll(ids, zh * ROWS, 1), 0)
    for cp in copies[2:7]:
        cp.wait()
    pl.semaphore_wait(barrier, len(near))

    right, left = dev(dz=1), dev(dz=-1)
    outward, inward = dev(dz=2 * zl - 1), dev(dz=1 - 2 * zl)
    xr, xl = dev(dx=1), dev(dx=-1)
    yu, yd = dev(dy=1), dev(dy=-1)
    z_near, z_away = (1 - zl) * zm + zl * zp, (1 - zl) * zp + zl * zm
    zz = (zm, zp, zo)

    v_z = (1 - zl) * 4 + y
    v_up, v_dn, v_far = zl * 4 + (y + 1) % 4, zl * 4 + (y + 3) % 4, zl * 4 + (y + 2) % 4
    w_up, w_dn, w_far = (1 - zl) * 4 + (y + 1) % 4, (1 - zl) * 4 + (y + 3) % 4, (1 - zl) * 4 + (y + 2) % 4
    features = (v, v_z, v_dn, v_up, v_far, w_dn, w_up, w_far)

    block = {}

    def small(vv, xx, zq):
        return r.at[vv, c, xx, :, zq]

    for k in range(3):
        block["sz", k] = small(v, x, zz[k])
        block["sx", k] = small(v, (xm, xp, xo)[k], zh)
        block["mz", k] = meta.at[c, x, zz[k]]
        block["mx", k] = meta.at[c, (xm, xp, xo)[k]]
        block["s2l", k] = small(v, xm, zz[k])
        block["s2r", k] = small(v, xp, zz[k])
        block["s3l", k] = r.at[v, c, xo, 0, zz[k]]
        block["s3r", k] = r.at[v, c, xo, 1, zz[k]]
    block["ms", 0] = meta.at[1 - c]
    block["w", 0] = w.at[COLS:]
    order = [(x, zh)] + [(x, q) for q in zz] + [(xx, zh) for xx in xg[1:]] + [(xx, q) for xx in xg[1:] for q in zz]
    for k, (xx, zq) in enumerate(order):
        block["yu", k] = small(v_dn, xx, zq)
        block["yd", k] = small(v_up, xx, zq)
    for g in range(4):
        block["rr", g] = r.at[v_z, c, xg[g], 0]
        block["rl", g] = r.at[v_z, c, xg[g], 1]
        block["cu", g] = r.at[w_dn, c, xg[g]]
        block["cd", g] = r.at[w_up, c, xg[g]]
        block["fu", g] = r.at[v_far, c, xg[g], 1]
        block["fd", g] = r.at[v_far, c, xg[g], 0]
        block["lr", g] = r.at[w_far, c, xg[g], 0]
        block["ll", g] = r.at[w_far, c, xg[g], 1]
    for k in range(8):
        block["v", k] = r.at[features[k], 1 - c]

    def qn(k):
        return zl * (3 - k) + (1 - zl) * k

    def qf(k):
        return zl * k + (1 - zl) * (3 - k)

    def near_block(xx, k):
        return t.at[xx, z_near if k < 4 else zo, qn(k % 4)]

    def away_block(xx, k):
        return t.at[xx, z_away if k < 4 else zo, qf(k % 4)]

    quarter = {}
    for k in range(6):
        for g, xx in enumerate((x, xo)):
            block["tn%d" % g, k] = near_block(xx, k)
            block["tf%d" % g, k] = away_block(xx, k)
            quarter["tn%d" % g, k] = 3 - k % 4
            quarter["tf%d" % g, k] = k % 4
        for name, xx in (("tl", xm), ("tr", xp)):
            block[name, 4 + 2 * k] = near_block(xx, k)
            block[name, 5 + 2 * k] = away_block(xx, k)
            quarter[name, 4 + 2 * k] = 3 - k % 4
            quarter[name, 5 + 2 * k] = k % 4
    for k in range(4):
        block["tl", k] = t.at[xm, zh, qf(k)]
        block["tr", k] = t.at[xp, zh, qf((k + 2) % 4)]
        quarter["tl", k] = k
        quarter["tr", k] = (k + 2) % 4
    for k in range(2):
        block["ul", k] = t.at[xo, zh, qf(k)]
        block["ur", k] = t.at[xo, zh, qf(k + 2)]
        quarter["ul", k] = k
        quarter["ur", k] = k + 2
    def wait_key(name, k):
        if name in ("yu", "yd"):
            g = [n for n in range(4) if k in members[n]][0]
            return (name, g), r.at[v_dn if name == "yu" else v_up, c, xg[g]]
        if name in ("rr", "rl"):
            return ("rr", k), r.at[v_z, c, xg[k]]
        if name in ("fu", "fd"):
            return ("fu", k), r.at[v_far, c, xg[k]]
        if name in ("s3l", "s3r"):
            return ("s3l", k), small(v, xo, zz[k])
        if name in ("cu", "cd"):
            return (name, 0), r.at[w_dn if name == "cu" else w_up, c]
        if name in ("lr", "ll"):
            return ("lr", 0), r.at[w_far, c]
        if name == "mz":
            return (name, 0), meta.at[c, x, pl.ds(0, 3)]
        if name == "mx":
            return (name, 0), meta.at[c, pl.ds(0, 3)]
        if name in ("tl", "tr") and k >= 4:
            return ("tq", quarter[name, k]), t.at[0, pl.ds(0, 3), pl.ds(0, 2)]
        return (name, k), block[name, k]

    members = ((0, 1, 2, 3), (4, 7, 8, 9), (5, 10, 11, 12), (6, 13, 14, 15))
    wait_of = {name: wait_key(*name) for name in block}
    keys = {}
    for key, _ in wait_of.values():
        keys.setdefault(key, len(keys))
    assert len(keys) == ARRIVALS, len(keys)

    sent = {n: 0 for n in range(11)}
    waited = set()

    def send_sem(name):
        if name in ("v", "w"):
            n = 0 if name == "v" else 1
        elif name in ("rr", "rl", "cu", "cd", "fu", "fd", "lr", "ll"):
            n = 4
        elif name in ("s3l", "s3r"):
            n = 7
        elif name in ("mz", "mx", "ms"):
            n = 8 + ("mz", "mx", "ms").index(name)
        elif name in ("sz", "sx", "s2l", "s2r", "yu", "yd"):
            n = 5 if sent[5] < 32 else 6
        else:
            n = 2 if sent[2] < 48 else 3
        sent[n] += 1
        return n

    def put(name, n, ref, to, dst=None):
        pltpu.make_async_remote_copy(
            src_ref=ref, dst_ref=ref if dst is None else dst, send_sem=ssem.at[send_sem(name)],
            recv_sem=rsem.at[keys[wait_of[name, n][0]]], device_id=to, device_id_type=MESH).start()

    def all_sent():
        whole_sends = (
            r.at[:, 0], w.at[:COLS], t.at[pl.ds(0, 3)], t.at[0, pl.ds(0, 3)], r.at[pl.ds(0, 5), 0],
            r.at[:, 0, :, :, 0], r.at[pl.ds(0, 3), 0, :, :, 0], r.at[pl.ds(0, 3), 0, 0, :, 0],
            meta.at[0, 0, pl.ds(0, 3)], meta.at[0, pl.ds(0, 3)], meta.at[0],
        )
        assert tuple(sent.values()) == (8, 1, 48, 12, 32, 32, 12, 6, 3, 3, 1), sent
        for n, ref in enumerate(whole_sends):
            pltpu.make_async_remote_copy(
                src_ref=ref, dst_ref=ref, send_sem=ssem.at[n], recv_sem=ssem.at[n],
                device_id=partner, device_id_type=MESH).wait_send()

    def need(*names):
        for name in names:
            key, ref = wait_of[name]
            if key not in waited:
                waited.add(key)
                sem = rsem.at[keys[key]]
                pltpu.make_async_remote_copy(
                    src_ref=ref, dst_ref=ref, send_sem=sem, recv_sem=sem,
                    device_id=partner, device_id_type=MESH).wait_recv()

    def up_down(k, ref):
        put("yu", k, ref, yu)
        put("yd", k, ref, yd)

    own = small(v, x, zh)
    of_group = (
        [("sz", k) for k in range(3)],
        [("sx", 0)] + [("s2l", k) for k in range(3)],
        [("sx", 1)] + [("s2r", k) for k in range(3)],
        [("sx", 2)] + [(a, k) for a in ("s3l", "s3r") for k in range(3)],
    )
    whole = (
        sum(of_group, []),
        [(a, g) for a in ("rr", "rl") for g in range(4)],
        [("yu", k) for k in range(16)],
        [("yd", k) for k in range(16)],
        [(a, g) for a in ("fu", "fd") for g in range(4)],
        [("cu", g) for g in range(4)],
        [("cd", g) for g in range(4)],
        [(a, g) for a in ("lr", "ll") for g in range(4)],
    )

    def do(task, k):
        if task == "start":
            for n, d in enumerate((2, -2, 4)):
                put("sz", n, own, dev(dz=d))
            for n, d in enumerate((1, -1, 2)):
                put("sx", n, own, dev(dx=d))
            up_down(0, own)
            for n, d in enumerate((2, -2, 4)):
                put("mz", n, meta.at[c, x, zh], dev(dz=d))
        elif task == "head":
            copies[7].wait()
            put("w", 0, w.at[:COLS], partner, w.at[COLS:])
        elif task == "fx" and k < 4:
            put("tl", k, t.at[x, zh, qf(k)], xr)
            put("tr", k, t.at[x, zh, qf((k + 2) % 4)], xl)
        elif task == "fx":
            name = ("tf0", (k - 5) // 2) if k % 2 else ("tn0", (k - 4) // 2)
            need(name)
            put("tl", k, block[name], xr)
            put("tr", k, block[name], xl)
        elif task == "tzown":
            put("tn0", k, t.at[x, zh, qf(k)], outward)
        elif task == "meta1":
            need(("mz", 0), ("mz", 1), ("mz", 2))
            for n, d in enumerate((1, -1, 2)):
                put("mx", n, meta.at[c, x], dev(dx=d))
        elif task == "meta2":
            need(("mx", 0), ("mx", 1), ("mx", 2))
            put("ms", 0, meta.at[c], partner)
        elif task == "sz":
            need(("sz", k))
            ref = block["sz", k]
            put("s2l", k, ref, xr)
            put("s2r", k, ref, xl)
            up_down(1 + k, ref)
        elif task == "sx":
            need(("sx", k))
            up_down(4 + k, block["sx", k])
        elif task == "s2l":
            need(("s2l", k))
            put("s3l", k, r.at[v, c, xm, 0, zz[k]], xr)
            up_down(7 + k, block["s2l", k])
        elif task == "s2r":
            need(("s2r", k))
            put("s3r", k, r.at[v, c, xp, 1, zz[k]], xl)
            up_down(10 + k, block["s2r", k])
        elif task == "s3":
            need(("s3l", k), ("s3r", k))
            up_down(13 + k, small(v, xo, zz[k]))
        elif task == "spread":
            need(*of_group[k])
            put("rr", k, r.at[v, c, xg[k], 0], right)
            put("rl", k, r.at[v, c, xg[k], 1], left)
        elif task == "cross":
            need(("rr", k), ("rl", k))
            put("cu", k, r.at[v_z, c, xg[k]], yu)
            put("cd", k, r.at[v_z, c, xg[k]], yd)
        elif task == "relayu":
            need(*[("yu", i) for i in members[k]])
            put("fu", k, r.at[v_dn, c, xg[k], 1], yu)
        elif task == "relayd":
            need(*[("yd", i) for i in members[k]])
            put("fd", k, r.at[v_up, c, xg[k], 0], yd)
        elif task == "far":
            need(("fu", k), ("fd", k))
            put("lr", k, r.at[v_far, c, xg[k], 0], right)
            put("ll", k, r.at[v_far, c, xg[k], 1], left)
        elif task == "swap":
            need(*whole[k])
            put("v", k, r.at[features[k], c], partner)
        elif task in ("near0", "near1"):
            g = task[-1]
            need(("tn" + g, k))
            ref = block["tn" + g, k]
            put("tf" + g, k, ref, inward)
        elif task in ("away0", "away1"):
            g = task[-1]
            need(("tf" + g, k))
            put("tn" + g, 4 + k, block["tf" + g, k], outward)
        elif task == "tl":
            need(("tl", k))
            put("ul", k, block["tl", k], xr)
        elif task == "tr":
            need(("tr", k))
            put("ur", k, block["tr", k], xl)
        elif task == "own1":
            name = ("ul", k) if k < 2 else ("ur", k - 2)
            need(name)
            put("tn1", k, block[name], outward)
        elif task == "R":
            need(("v", k), ("w", 0), *whole[k])
            rollout_part(features[k])
        elif task == "T":
            need(("w", 0), *[name for name, q in quarter.items() if q == k])
            trainer_part(qf(k))
        elif task == "onehot":
            need(("ms", 0))
            fill_onehot()
        elif task == "TS":
            lax.fori_loop(0, NX, train_stats, 0)
        elif task == "RS":
            lax.fori_loop(0, NX, roll_stats, 0)

    def fill_onehot():
        place = lax.broadcasted_iota(jnp.int32, (TOK, GROUP), 0)
        for cc in range(2):
            for xx in range(NX):
                slot = meta[cc, xx, 0, 0:1, :]
                for zq in range(1, NH):
                    slot = slot + meta[cc, xx, zq, 0:1, :]
                token = (slot >> 6) * ROWS + (slot & (ROWS - 1))
                token = jnp.where(((slot >> 5) & 1) == c, token, -1)
                n = cc * NX + xx
                onehot[:, n * GROUP:(n + 1) * GROUP] = jnp.where(place == token, 1.0, 0.0).astype(BF16)

    def logits(rows, f):
        return lax.dot_general(rows, w[:, f], (((1,), (1,)), ((), ())), preferred_element_type=F32)

    begun = set()

    def add(logit, part):
        if id(logit) in begun:
            logit[...] += part
        else:
            begun.add(id(logit))
            logit[...] = part

    def rollout_part(vv):
        rows = r[vv].reshape(2 * TOK, FEAT)
        perm[...] = jnp.dot(onehot[...], rows, preferred_element_type=F32).astype(BF16)
        add(lr, logits(perm[...], pl.ds(pl.multiple_of(vv * FEAT, FEAT), FEAT)))

    def trainer_part(q):
        rows = t[:, :, pl.ds(q, 1)].reshape(TOK, PART)
        add(lt, logits(rows, pl.ds(pl.multiple_of(q * PART, PART), PART)))

    lane = lax.broadcasted_iota(jnp.int32, (GROUP, 128), 1)
    column = lax.broadcasted_iota(jnp.int32, (GROUP, 2 * COLS), 1)
    column = column + jnp.where(column < COLS, (s * 8 + v) * COLS, ((s + 1 - 2 * c) * 8 + v) * COLS - COLS)
    diagonal = lax.broadcasted_iota(jnp.int32, (GROUP, 128), 0) == lane

    def local_stats(logit, stat, xx, rows):
        ids = meta[c, xx, 0, 1:2, :]
        for zq in range(1, NH):
            ids = ids + meta[c, xx, zq, 1:2, :]
        ids = jnp.sum(jnp.where(diagonal, ids, 0), axis=1, keepdims=True)
        values = logit[rows]
        top = jnp.max(values, axis=1, keepdims=True)
        e = jnp.exp(values - top)
        logit[rows] = e
        total = jnp.sum(e, axis=1, keepdims=True)
        pick = jnp.sum(jnp.where(column == ids, values, 0.0), axis=1, keepdims=True)
        table = jnp.where(lane == 0, top, jnp.where(lane == 1, total, jnp.where(lane == 2, pick, 0.0)))
        stat[xx] = jnp.transpose(table)[:8]

    rows_of = lambda xx: pl.ds(pl.multiple_of(xx * GROUP, GROUP), GROUP)

    def train_stats(xx, carry):
        local_stats(lt, stat_t, xx, rows_of(xx))
        return carry

    def roll_stats(xx, carry):
        local_stats(lr, stat_r, xx, rows_of(xx))
        return carry

    def exchange(buf, count, sem, to):
        def start(d, carry):
            pltpu.make_async_remote_copy(
                src_ref=buf.at[0], dst_ref=buf.at[d], send_sem=a_sem.at[sem], recv_sem=a_sem.at[sem + 1],
                device_id=to(d), device_id_type=MESH).start()
            return carry
        lax.fori_loop(1, count, start, 0)
        rest = buf.at[pl.ds(1, count - 1)]
        return pltpu.make_async_remote_copy(
            src_ref=rest, dst_ref=rest, send_sem=a_sem.at[sem], recv_sem=a_sem.at[sem + 1],
            device_id=partner, device_id_type=MESH)

    def merge(buf, count):
        top = buf[0, 0]
        for d in range(1, count):
            top = jnp.maximum(top, buf[d, 0])
        total = jnp.zeros_like(top)
        for d in range(count):
            total = total + buf[d, 1] * jnp.exp(buf[d, 0] - top)
        return top, total

    def plane(n, stat):
        a1[n, 0, 0] = stat[:, 0, :]
        a1[n, 0, 1] = stat[:, 1, :]
        return exchange(a1.at[n], 16, 4 * n, lambda d: dev(dx=d // 4, dy=d % 4))

    def column_z(n, before):
        before.wait_recv()
        top, total = merge(a1.at[n], 16)
        a2[n, 0, 0] = top
        a2[n, 0, 1] = total
        return exchange(a2.at[n], 8, 4 * n + 2, lambda d: dev(dz=d))

    def finish(n, before):
        before.wait_recv()
        top, total = merge(a2.at[n], 8)
        fin[n, 0] = top
        fin[n, 1] = total

    for task, k in ORDER:
        do(task, k)
        if task == "TS":
            plane_t = plane(1, stat_t)
    plane_r = plane(0, stat_r)
    column_t = column_z(1, plane_t)
    column_r = column_z(0, plane_r)
    finish(1, column_t)
    finish(0, column_r)

    def compare(xx, carry):
        rows = pl.ds(pl.multiple_of(xx * GROUP, GROUP), GROUP)
        scale_r = jnp.exp(stat_r[xx, 0:1, :] - fin[0, 0, pl.ds(xx, 1), :]) / fin[0, 1, pl.ds(xx, 1), :]
        scale_t = jnp.exp(stat_t[xx, 0:1, :] - fin[1, 0, pl.ds(xx, 1), :]) / fin[1, 1, pl.ds(xx, 1), :]
        scale_r = jnp.sum(jnp.where(diagonal, scale_r, 0.0), axis=1, keepdims=True)
        scale_t = jnp.sum(jnp.where(diagonal, scale_t, 0.0), axis=1, keepdims=True)
        p = lr[rows, :] * scale_r
        q = lt[rows, :] * scale_t
        shared = jnp.sum(jnp.minimum(p, q), axis=1, keepdims=True)
        squares = jnp.sum((q - p) * (q - p), axis=1, keepdims=True)
        table = jnp.where(lane == 0, shared, jnp.where(lane == 1, squares, 0.0))
        table = jnp.transpose(table)[:2]
        values = (table[0:1], table[1:2], stat_r[xx, 2:3, :], stat_t[xx, 2:3, :])
        part = lax.broadcasted_iota(jnp.int32, (1, 128), 1) // ROWS
        for zq in range(NH):
            one = jnp.zeros((1, 128), F32)
            for k in range(4):
                one = one + jnp.where(part == k, pltpu.roll(values[k], ((k - zq) % 4) * ROWS, 1), 0.0)
            out2[xx, zq] = one
        return carry
    lax.fori_loop(0, NX, compare, 0)

    a3[0] = out2[x, zh]

    def send(d, carry):
        dx, dy, dz = d // 32, (d // 8) % 4, d % 8
        pltpu.make_async_remote_copy(
            src_ref=out2.at[(x + dx) % NX, ((z + dz) % NZ) // 2], dst_ref=a3.at[d],
            send_sem=a_sem.at[8], recv_sem=a_sem.at[9], device_id=dev(dx, dy, dz), device_id_type=MESH).start()
        return carry
    lax.fori_loop(1, 128, send, 0)
    rest = a3.at[pl.ds(1, 127)]
    done3 = pltpu.make_async_remote_copy(
        src_ref=rest, dst_ref=rest, send_sem=a_sem.at[8], recv_sem=a_sem.at[9],
        device_id=partner, device_id_type=MESH)
    all_sent()
    for done in (plane_t, plane_r, column_t, column_r):
        done.wait_send()
    done3.wait_recv()
    sums = jnp.sum(a3[...], axis=0)
    shift = (NH - zh) % NH * ROWS
    own_top = [pltpu.roll(fin[n, 0, pl.ds(x, 1), :], shift, 1)[:, :ROWS] for n in range(2)]
    own_total = [pltpu.roll(fin[n, 1, pl.ds(x, 1), :], shift, 1)[:, :ROWS] for n in range(2)]
    pick_r = pltpu.roll(sums, 2 * ROWS, 1)[:, :ROWS]
    pick_t = pltpu.roll(sums, ROWS, 1)[:, :ROWS]
    squares = pltpu.roll(sums, 3 * ROWS, 1)[:, :ROWS]
    log_ratio = pick_t - own_top[1] - jnp.log(own_total[1]) - (pick_r - own_top[0] - jnp.log(own_total[0]))
    out[0:1, :] = sums[:, :ROWS]
    out[1:2, :] = jnp.sqrt(squares + 1e-06)
    out[2:3, :] = jnp.minimum(jnp.exp(log_ratio), 2.0)
    done3.wait_send()


def per_device(rollout_hidden, trainer_hidden, head_weight, token_ids, response_mask, trainer_slot):
    dma, reg = pltpu.SemaphoreType.DMA, pl.BlockSpec(memory_space=pl.ANY)
    vmem = pl.BlockSpec(memory_space=pltpu.VMEM)
    sums = pl.pallas_call(
        kernel,
        out_shape=jax.ShapeDtypeStruct((3, ROWS), F32),
        in_specs=[reg] * 5,
        out_specs=vmem,
        scratch_shapes=[
            pltpu.VMEM((2 * COLS, D), BF16),
            pltpu.VMEM((NX, NH, 4, ROWS, PART), BF16),
            pltpu.VMEM((8, 2, NX, 2, NH, HALF, FEAT), BF16),
            pltpu.VMEM((1, ROWS), jnp.int32),
            pltpu.VMEM((1, ROWS), jnp.int32),
            pltpu.VMEM((2, 128), jnp.int32),
            pltpu.VMEM((2, NX, NH, 2, 128), jnp.int32),
            pltpu.VMEM((TOK, 2 * TOK), BF16),
            pltpu.VMEM((TOK, FEAT), BF16),
            pltpu.VMEM((TOK, 2 * COLS), F32),
            pltpu.VMEM((TOK, 2 * COLS), F32),
            pltpu.VMEM((NX, 8, 128), F32),
            pltpu.VMEM((NX, 8, 128), F32),
            pltpu.VMEM((2, 16, 2, NX, 128), F32),
            pltpu.VMEM((2, 8, 2, NX, 128), F32),
            pltpu.VMEM((2, 2, NX, 128), F32),
            pltpu.VMEM((NX, NH, 1, 128), F32),
            pltpu.VMEM((128, 1, 128), F32),
            dma((11,)), dma((ARRIVALS,)), dma((8,)), dma((10,)),
        ],
        compiler_params=pltpu.CompilerParams(
            collective_id=0, has_side_effects=True, vmem_limit_bytes=60 * 1024 * 1024),
        cost_estimate=pl.CostEstimate(
            flops=2 * 2 * TOK * D * 2 * COLS + 2 * TOK * 2 * TOK * D, bytes_accessed=D * COLS * 2, transcendentals=2 * TOK * 2 * COLS),
    )(rollout_hidden.reshape(2, HALF, FEAT), trainer_hidden, head_weight.T,
      trainer_slot.reshape(1, ROWS), token_ids.reshape(1, ROWS))
    mask = response_mask.astype(F32)
    return tuple(sums[n] * mask for n in range(3))


def solution(mesh):
    placed = (
        P("seq", "vocab"),
        P("seq", None),
        P(None, ("seq", "vocab")),
        P("seq"),
        P("seq"),
        P("seq"),
    )
    return jax.shard_map(
        per_device,
        mesh=mesh,
        in_specs=placed,
        out_specs=(P("seq"), P("seq"), P("seq")),
        check_vma=False,
    )
```

time: 447 us -> 84.2 us (0.19)
  blocking collectives: 274 us -> 0 us
  waiting for transfers between devices: 116 us -> 0 us
  Pallas kernels: 0 us -> 82.1 us
  matrix products: 22.3 us -> 0 us
  between operations: 14.8 us -> 0.66 us
  local copies, waits for them, and re-layouts: 11.3 us -> 0.01 us
  other arithmetic: 6.4 us -> 1.29 us
    psum x2 -> x0, blocking collectives: 148 us -> none  [the longest x1 74.2 us: per_device(): lax.psum((jnp.sum(jnp.exp(roll_values - top_roll[:, None]), axis=1), jnp....]
    all_gather x2 -> x0, waiting for transfers between devices: 116 us -> none  [the longest x1 59.5 us: per_device(): train_rows = lax.all_gather(trainer_hidden, 'seq', axis=0, tiled=True)]
    pallas_call x0 -> x1, Pallas kernels: none -> 82.1 us  [per_device(): pl.pallas_call(kernel, out_shape=jax.ShapeDtypeStruct((3, ROWS), F32), in...]
    pmax x1 -> x0, blocking collectives: 75.1 us -> none  [per_device(): top_roll, top_train = lax.pmax((local_roll, local_train), ('seq', 'vocab'))]
    all_gather x1 -> x0, blocking collectives: 31.6 us -> none  [per_device(): whole_rows = lax.all_gather(rollout_hidden, 'vocab', axis=1, tiled=True)]
    dot_general x2 -> x0, matrix products: 22.3 us -> none  [the longest x1 11.6 us: per_device(): jnp.dot(roll_rows, head_weight, preferred_element_type=jnp.float32)]
    unnamed x1 -> x0, blocking collectives: 19.5 us -> none
    scatter x2 -> x0, local copies, waits for them, and re-layouts: 8.3 us -> none  [per_device(): roll_state.at[slots].set(roll_part)]
  transfers between devices with their start and end apart: 2 -> 0, of which waited for: 2 -> 0; matrix products, arithmetic and copies ran while one was open for 5% -> 0% of each run, Pallas kernels for 0% -> 0%
where the time goes in v2:
time: 84.2 us; the launch traced here: 84.1 us
  Pallas kernels  82.1 us (98%)
  other arithmetic  1.29 us (2%)
    pallas_call x1, Pallas kernels, per_device(): pl.pallas_call(kernel, out_shape=jax.ShapeDtypeStruct((3, ROWS), F32), in...  82.1 us

profile of v2, /device:TPU:2, one launch (start us, length us, event | category | flops | bytes accessed | tf_op | source)
XLA Modules:
  0.0 84.1 jit_solution(3145030298874034513)
XLA Ops:
  0.6 0.0 copy-start
  0.6 82.1 %shard_map.85 = f32[3,32]{1,0:T(4,128)} custom-call(bf16[2,16,512]{2,1,0:T(8,128)(2,1)} %bitcast.11, bf16[32,4096]{1,0:T(8,128)(2,1)} %train_in.1, bf16[592,4096]{1,0:T(8,128)(2,1)} %bitcast.10, s32[1,32]{1,0:T(1,128)} %bitcast.12, s32[1,32]{1,0:T(1,128)} %bitcast.13), custom_call_target="tpu_custom_call" | custom-call | flops 14227079168 | bytes 4849664 | tf_op jit(solution)/shard_map/pallas_call | solution.py:536
  82.8 0.0 copy-done
  82.8 1.3 %bitcast_multiply_fusion = (f32[32]{0:T(128)}, f32[32]{0:T(128)}, f32[32]{0:T(128)}) fusion(f32[3,32]{1,0:T(4,128)} %shard_map.85, s32[32]{0:T(128)S(1)} %copy-done), kind=kLoop, calls=%fused_computation | loop fusion | flops 128 | bytes 896 | tf_op jit(solution)/shard_map/mul | solution.py:569
Async XLA Ops:
  0.6 82.2 %copy-start = (s32[32]{0:T(128)S(1)}, s32[32]{0:T(128)}, u32[]{:S(2)}) copy-start(s32[32]{0:T(128)} %param.10) | copy-start | bytes 388

commit v3 on v2

--- a/solution.py
+++ b/solution.py
@@ -14,49 +14,63 @@
 D = 4096
 FEAT = 512
 COLS = 592
+WIDE = 1280
 TOK = 512
 GROUP = 128
 PART = 1024
 ARRIVALS = 86
 
 ORDER = (
-    ("start", 0), ("fx", 1), ("tzown", 1), ("fx", 3), ("tzown", 0), ("sx", 0),
-    ("sx", 1), ("fx", 0), ("head", 0), ("tzown", 3), ("sx", 2), ("sz", 1),
-    ("tl", 1), ("tr", 1), ("tzown", 2), ("near0", 1), ("sz", 0), ("spread", 0),
-    ("meta1", 0), ("sz", 2), ("tr", 0), ("tl", 0), ("near0", 0), ("s2r", 1),
-    ("s2l", 1), ("near0", 3), ("fx", 10), ("own1", 1), ("own1", 3), ("relayu", 0),
-    ("relayd", 0), ("near0", 2), ("fx", 8), ("meta2", 0), ("away0", 1), ("cross", 0),
-    ("fx", 4), ("own1", 2), ("near1", 1), ("onehot", 0), ("s2l", 0), ("fx", 5),
-    ("own1", 0), ("s3", 1), ("near1", 3), ("s2r", 0), ("fx", 6), ("away0", 0),
-    ("near0", 5), ("s2r", 2), ("s2l", 2), ("spread", 2), ("fx", 9), ("near1", 2),
-    ("away1", 1), ("fx", 14), ("s3", 0), ("near1", 0), ("fx", 2), ("relayu", 2),
-    ("relayd", 2), ("swap", 0), ("s3", 2), ("spread", 3), ("relayu", 1), ("relayd", 1),
-    ("fx", 12), ("spread", 1), ("cross", 2), ("fx", 15), ("R", 0), ("near0", 4),
-    ("away1", 0), ("fx", 7), ("swap", 2), ("swap", 3), ("T", 2), ("far", 1),
-    ("relayd", 3), ("relayu", 3), ("fx", 11), ("near1", 5), ("R", 2), ("near1", 4),
-    ("swap", 1), ("cross", 1), ("R", 3), ("far", 2), ("fx", 13), ("cross", 3),
-    ("swap", 4), ("T", 3), ("far", 3), ("R", 1), ("far", 0), ("T", 1),
-    ("R", 4), ("swap", 5), ("swap", 6), ("T", 0), ("TS", 0), ("swap", 7),
-    ("R", 5), ("R", 6), ("R", 7), ("RS", 0),
+    ("fx", 0), ("start", 0), ("fx", 1), ("tzown", 0), ("fx", 3), ("tzown", 2),
+    ("tl", 0), ("tr", 0), ("tzown", 1), ("sx", 0), ("yz", 0), ("head", 0),
+    ("yz", 1), ("sx", 1), ("sz", 0), ("tzown", 3), ("sx", 2), ("sz", 1),
+    ("near0", 0), ("tl", 1), ("tr", 1), ("spread", 0), ("yz", 2), ("near0", 2),
+    ("meta1", 0), ("fx", 4), ("own1", 0), ("near0", 1), ("sz", 2), ("own1", 2),
+    ("y2l", 0), ("y2r", 0), ("s2r", 0), ("s2l", 0), ("fx", 5), ("y2r", 1),
+    ("near0", 3), ("y2l", 1), ("away0", 0), ("relayu", 0), ("relayd", 0), ("s2r", 1),
+    ("s2l", 1), ("fx", 6), ("own1", 3), ("cross", 0), ("meta2", 0), ("near1", 0),
+    ("fx", 9), ("own1", 1), ("onehot", 0), ("near1", 2), ("s2r", 2), ("s2l", 2),
+    ("spread", 2), ("y2r", 2), ("fx", 7), ("s3", 0), ("near0", 4), ("away0", 1),
+    ("y2l", 2), ("fx", 11), ("s3", 1), ("near1", 3), ("away1", 0), ("fx", 12),
+    ("near1", 1), ("swap", 0), ("s3", 2), ("fx", 10), ("relayu", 2), ("relayd", 2),
+    ("spread", 1), ("cross", 2), ("fx", 2), ("R", 0), ("swap", 2), ("relayu", 1),
+    ("relayd", 1), ("fx", 13), ("spread", 3), ("near1", 4), ("swap", 3), ("T", 3),
+    ("relayu", 3), ("near0", 5), ("relayd", 3), ("away1", 1), ("fx", 14), ("fx", 8),
+    ("R", 2), ("far", 2), ("cross", 1), ("swap", 1), ("R", 3), ("far", 0),
+    ("cross", 3), ("far", 1), ("T", 0), ("near1", 5), ("fx", 15), ("swap", 4),
+    ("T", 2), ("far", 3), ("R", 1), ("R", 4), ("swap", 5), ("swap", 6),
+    ("T", 1), ("TS", 0), ("swap", 7), ("R", 5), ("R", 6), ("R", 7),
+    ("RS", 0),
 )
 
 
 def kernel(roll_in, train_in, head_in, slot_in, ids_in, out,
-           w, t, r, slot_v, ids_v, line, meta, onehot, perm, lt, lr, stat_r, stat_t, a1, a2, fin, out2, a3,
+           w, t, r, slot_v, ids_v, line, meta, onehot, perm, lt, lr, et, er, stat_r, stat_t, a1, a2, fin, out2, a3,
            ssem, rsem, in_sem, a_sem):
     s, v = lax.axis_index("seq"), lax.axis_index("vocab")
-    x, zh, c = s // 8, (s // 2) % 4, s % 2
-    zl, y = v // 4, v % 4
+    x, zh, c = lax.div(s, 8), lax.rem(lax.div(s, 2), 4), lax.rem(s, 2)
+    zl, y = lax.div(v, 4), lax.rem(v, 4)
     z = zh * 2 + zl
 
+    x_at = [lax.rem(x + d, NX) for d in range(NX)]
+    y_at = [lax.rem(y + d, NY) for d in range(NY)]
+    z_at = [lax.rem(z + d, NZ) for d in range(NZ)]
+    zh_at = [lax.div(zz, 2) for zz in z_at]
+    seq_x = [8 * xx + c for xx in x_at]
+    seq_z = [2 * zz for zz in zh_at]
+    vocab_z = [4 * lax.rem(zz, 2) for zz in z_at]
+
     def dev(dx=0, dy=0, dz=0):
-        xx, yy, zz = (x + dx + NX) % NX, (y + dy + NY) % NY, (z + dz + NZ) % NZ
-        return ((xx * 4 + zz // 2) * 2 + c, (zz % 2) * 4 + yy)
+        return (seq_x[dx % NX] + seq_z[dz % NZ], vocab_z[dz % NZ] + y_at[dy % NY])
+
+    def offsets(xs, ys, zs):
+        every = [(dx, dy, dz) for dx in range(xs) for dy in range(ys) for dz in range(zs)][1:]
+        return sorted(every, key=lambda o: -min(o[0], NX - o[0]) - min(o[1], NY - o[1]) - min(o[2], NZ - o[2]))
 
     partner = (s + 1 - 2 * c, v)
-    xm, xp, xo = (x + 3) % 4, (x + 1) % 4, (x + 2) % 4
+    xm, xp, xo = x_at[3], x_at[1], x_at[2]
     xg = (x, xm, xp, xo)
-    zm, zp, zo = (zh + 3) % 4, (zh + 1) % 4, (zh + 2) % 4
+    zm, zp, zo = zh_at[6], zh_at[2], zh_at[4]
 
     barrier = pltpu.get_barrier_semaphore()
     near = [dev(dz=d) for d in (4, 2, -2)] + [dev(dx=2)] + [dev(dx=d) for d in (1, -1)]
@@ -84,20 +98,24 @@
     high = jnp.where(lanes // HALF == NH + zh, pltpu.roll(slots, (NH - 1 + zh) * HALF, 1), 0)
     meta[c, x, zh, 0:1, :] = low + high
     meta[c, x, zh, 1:2, :] = jnp.where(lanes // ROWS == zh, pltpu.roll(ids, zh * ROWS, 1), 0)
+    edge = pl.ds(WIDE - 128, 128)
+    lt[:, edge] = jnp.full((TOK, 128), -jnp.inf, F32)
+    lr[:, edge] = jnp.full((TOK, 128), -jnp.inf, F32)
     for cp in copies[2:7]:
         cp.wait()
     pl.semaphore_wait(barrier, len(near))
 
     right, left = dev(dz=1), dev(dz=-1)
-    outward, inward = dev(dz=2 * zl - 1), dev(dz=1 - 2 * zl)
+    outward = tuple(zl * a + (1 - zl) * b for a, b in zip(right, left))
+    inward = tuple(zl * b + (1 - zl) * a for a, b in zip(right, left))
     xr, xl = dev(dx=1), dev(dx=-1)
     yu, yd = dev(dy=1), dev(dy=-1)
     z_near, z_away = (1 - zl) * zm + zl * zp, (1 - zl) * zp + zl * zm
     zz = (zm, zp, zo)
 
     v_z = (1 - zl) * 4 + y
-    v_up, v_dn, v_far = zl * 4 + (y + 1) % 4, zl * 4 + (y + 3) % 4, zl * 4 + (y + 2) % 4
-    w_up, w_dn, w_far = (1 - zl) * 4 + (y + 1) % 4, (1 - zl) * 4 + (y + 3) % 4, (1 - zl) * 4 + (y + 2) % 4
+    v_up, v_dn, v_far = [zl * 4 + y_at[d] for d in (1, 3, 2)]
+    w_up, w_dn, w_far = [(1 - zl) * 4 + y_at[d] for d in (1, 3, 2)]
     features = (v, v_z, v_dn, v_up, v_far, w_dn, w_up, w_far)
 
     block = {}
@@ -297,17 +315,23 @@
             ref = block["sz", k]
             put("s2l", k, ref, xr)
             put("s2r", k, ref, xl)
-            up_down(1 + k, ref)
+        elif task == "yz":
+            need(("sz", k))
+            up_down(1 + k, block["sz", k])
         elif task == "sx":
             need(("sx", k))
             up_down(4 + k, block["sx", k])
         elif task == "s2l":
             need(("s2l", k))
             put("s3l", k, r.at[v, c, xm, 0, zz[k]], xr)
+        elif task == "y2l":
+            need(("s2l", k))
             up_down(7 + k, block["s2l", k])
         elif task == "s2r":
             need(("s2r", k))
             put("s3r", k, r.at[v, c, xp, 1, zz[k]], xl)
+        elif task == "y2r":
+            need(("s2r", k))
             up_down(10 + k, block["s2r", k])
         elif task == "s3":
             need(("s3l", k), ("s3r", k))
@@ -385,10 +409,10 @@
 
     def add(logit, part):
         if id(logit) in begun:
-            logit[...] += part
+            logit[:, :2 * COLS] += part
         else:
             begun.add(id(logit))
-            logit[...] = part
+            logit[:, :2 * COLS] = part
 
     def rollout_part(vv):
         rows = r[vv].reshape(2 * TOK, FEAT)
@@ -400,41 +424,67 @@
         add(lt, logits(rows, pl.ds(pl.multiple_of(q * PART, PART), PART)))
 
     lane = lax.broadcasted_iota(jnp.int32, (GROUP, 128), 1)
-    column = lax.broadcasted_iota(jnp.int32, (GROUP, 2 * COLS), 1)
-    column = column + jnp.where(column < COLS, (s * 8 + v) * COLS, ((s + 1 - 2 * c) * 8 + v) * COLS - COLS)
     diagonal = lax.broadcasted_iota(jnp.int32, (GROUP, 128), 0) == lane
 
-    def local_stats(logit, stat, xx, rows):
+    def to_row(values):
+        return jnp.sum(jnp.where(diagonal, values, 0), axis=0, keepdims=True)
+
+    def to_column(values):
+        return jnp.sum(jnp.where(diagonal, values, 0), axis=1, keepdims=True)
+
+    def rows_of(xx):
+        return pl.ds(pl.multiple_of(xx * GROUP, GROUP), GROUP)
+
+    tiles = [pl.ds(128 * j, 128) for j in range(WIDE // 128)]
+
+    def group_stats(logit, ex, stat, xx):
+        rows = rows_of(xx)
+        top = logit[rows, tiles[0]]
+        for tile in tiles[1:]:
+            top = jnp.maximum(top, logit[rows, tile])
+        top = jnp.max(top, axis=1, keepdims=True)
+        total = jnp.zeros((GROUP, 128), F32)
+        for tile in tiles:
+            e = jnp.exp(logit[rows, tile] - top)
+            ex[rows, tile] = e
+            total = total + e
+        stat[xx, 0:1, :] = to_row(top)
+        stat[xx, 1:2, :] = to_row(jnp.sum(total, axis=1, keepdims=True))
+
+    def group_picks(logit, stat, xx):
+        rows = rows_of(xx)
         ids = meta[c, xx, 0, 1:2, :]
         for zq in range(1, NH):
             ids = ids + meta[c, xx, zq, 1:2, :]
-        ids = jnp.sum(jnp.where(diagonal, ids, 0), axis=1, keepdims=True)
-        values = logit[rows]
-        top = jnp.max(values, axis=1, keepdims=True)
-        e = jnp.exp(values - top)
-        logit[rows] = e
-        total = jnp.sum(e, axis=1, keepdims=True)
-        pick = jnp.sum(jnp.where(column == ids, values, 0.0), axis=1, keepdims=True)
-        table = jnp.where(lane == 0, top, jnp.where(lane == 1, total, jnp.where(lane == 2, pick, 0.0)))
-        stat[xx] = jnp.transpose(table)[:8]
-
-    rows_of = lambda xx: pl.ds(pl.multiple_of(xx * GROUP, GROUP), GROUP)
+        ids = to_column(ids)
+        pick = jnp.zeros((GROUP, 128), F32)
+        for n, tile in enumerate(tiles):
+            column = lanes + 128 * n
+            column = jnp.where(
+                column < COLS, column + (s * 8 + v) * COLS,
+                jnp.where(column < 2 * COLS, column + ((s + 1 - 2 * c) * 8 + v) * COLS - COLS, -1))
+            pick = pick + jnp.where(column == ids, logit[rows, tile], 0.0)
+        stat[xx, 2:3, :] = to_row(jnp.sum(pick, axis=1, keepdims=True))
 
     def train_stats(xx, carry):
-        local_stats(lt, stat_t, xx, rows_of(xx))
+        group_stats(lt, et, stat_t, xx)
+        group_picks(lt, stat_t, xx)
         return carry
 
     def roll_stats(xx, carry):
-        local_stats(lr, stat_r, xx, rows_of(xx))
+        group_stats(lr, er, stat_r, xx)
         return carry
 
-    def exchange(buf, count, sem, to):
-        def start(d, carry):
+    def roll_picks(xx, carry):
+        group_picks(lr, stat_r, xx)
+        return carry
+
+    def exchange(buf, sem, away):
+        count = len(away) + 1
+        for n, offset in enumerate(away):
             pltpu.make_async_remote_copy(
-                src_ref=buf.at[0], dst_ref=buf.at[d], send_sem=a_sem.at[sem], recv_sem=a_sem.at[sem + 1],
-                device_id=to(d), device_id_type=MESH).start()
-            return carry
-        lax.fori_loop(1, count, start, 0)
+                src_ref=buf.at[0], dst_ref=buf.at[n + 1], send_sem=a_sem.at[sem], recv_sem=a_sem.at[sem + 1],
+                device_id=dev(*offset), device_id_type=MESH).start()
         rest = buf.at[pl.ds(1, count - 1)]
         return pltpu.make_async_remote_copy(
             src_ref=rest, dst_ref=rest, send_sem=a_sem.at[sem], recv_sem=a_sem.at[sem + 1],
@@ -452,14 +502,14 @@
     def plane(n, stat):
         a1[n, 0, 0] = stat[:, 0, :]
         a1[n, 0, 1] = stat[:, 1, :]
-        return exchange(a1.at[n], 16, 4 * n, lambda d: dev(dx=d // 4, dy=d % 4))
+        return exchange(a1.at[n], 4 * n, offsets(NX, NY, 1))
 
     def column_z(n, before):
         before.wait_recv()
         top, total = merge(a1.at[n], 16)
         a2[n, 0, 0] = top
         a2[n, 0, 1] = total
-        return exchange(a2.at[n], 8, 4 * n + 2, lambda d: dev(dz=d))
+        return exchange(a2.at[n], 4 * n + 2, offsets(1, 1, NZ))
 
     def finish(n, before):
         before.wait_recv()
@@ -473,6 +523,7 @@
             plane_t = plane(1, stat_t)
     plane_r = plane(0, stat_r)
     column_t = column_z(1, plane_t)
+    lax.fori_loop(0, NX, roll_picks, 0)
     column_r = column_z(0, plane_r)
     finish(1, column_t)
     finish(0, column_r)
@@ -481,15 +532,17 @@
         rows = pl.ds(pl.multiple_of(xx * GROUP, GROUP), GROUP)
         scale_r = jnp.exp(stat_r[xx, 0:1, :] - fin[0, 0, pl.ds(xx, 1), :]) / fin[0, 1, pl.ds(xx, 1), :]
         scale_t = jnp.exp(stat_t[xx, 0:1, :] - fin[1, 0, pl.ds(xx, 1), :]) / fin[1, 1, pl.ds(xx, 1), :]
-        scale_r = jnp.sum(jnp.where(diagonal, scale_r, 0.0), axis=1, keepdims=True)
-        scale_t = jnp.sum(jnp.where(diagonal, scale_t, 0.0), axis=1, keepdims=True)
-        p = lr[rows, :] * scale_r
-        q = lt[rows, :] * scale_t
-        shared = jnp.sum(jnp.minimum(p, q), axis=1, keepdims=True)
-        squares = jnp.sum((q - p) * (q - p), axis=1, keepdims=True)
-        table = jnp.where(lane == 0, shared, jnp.where(lane == 1, squares, 0.0))
-        table = jnp.transpose(table)[:2]
-        values = (table[0:1], table[1:2], stat_r[xx, 2:3, :], stat_t[xx, 2:3, :])
+        scale_r, scale_t = to_column(scale_r), to_column(scale_t)
+        shared = jnp.zeros((GROUP, 128), F32)
+        squares = jnp.zeros((GROUP, 128), F32)
+        for tile in tiles:
+            p = er[rows, tile] * scale_r
+            q = et[rows, tile] * scale_t
+            shared = shared + jnp.minimum(p, q)
+            squares = squares + (q - p) * (q - p)
+        shared = to_row(jnp.sum(shared, axis=1, keepdims=True))
+        squares = to_row(jnp.sum(squares, axis=1, keepdims=True))
+        values = (shared, squares, stat_r[xx, 2:3, :], stat_t[xx, 2:3, :])
         part = lax.broadcasted_iota(jnp.int32, (1, 128), 1) // ROWS
         for zq in range(NH):
             one = jnp.zeros((1, 128), F32)
@@ -501,13 +554,10 @@
 
     a3[0] = out2[x, zh]
 
-    def send(d, carry):
-        dx, dy, dz = d // 32, (d // 8) % 4, d % 8
+    for n, (dx, dy, dz) in enumerate(offsets(NX, NY, NZ)):
         pltpu.make_async_remote_copy(
-            src_ref=out2.at[(x + dx) % NX, ((z + dz) % NZ) // 2], dst_ref=a3.at[d],
-            send_sem=a_sem.at[8], recv_sem=a_sem.at[9], device_id=dev(dx, dy, dz), device_id_type=MESH).start()
-        return carry
-    lax.fori_loop(1, 128, send, 0)
+            src_ref=out2.at[x_at[dx], zh_at[dz]], dst_ref=a3.at[n + 1], send_sem=a_sem.at[8], recv_sem=a_sem.at[9],
+            device_id=dev(dx, dy, dz), device_id_type=MESH).start()
     rest = a3.at[pl.ds(1, 127)]
     done3 = pltpu.make_async_remote_copy(
         src_ref=rest, dst_ref=rest, send_sem=a_sem.at[8], recv_sem=a_sem.at[9],
@@ -548,8 +598,10 @@
             pltpu.VMEM((2, NX, NH, 2, 128), jnp.int32),
             pltpu.VMEM((TOK, 2 * TOK), BF16),
             pltpu.VMEM((TOK, FEAT), BF16),
-            pltpu.VMEM((TOK, 2 * COLS), F32),
-            pltpu.VMEM((TOK, 2 * COLS), F32),
+            pltpu.VMEM((TOK, WIDE), F32),
+            pltpu.VMEM((TOK, WIDE), F32),
+            pltpu.VMEM((TOK, WIDE), F32),
+            pltpu.VMEM((TOK, WIDE), F32),
             pltpu.VMEM((NX, 8, 128), F32),
             pltpu.VMEM((NX, 8, 128), F32),
             pltpu.VMEM((2, 16, 2, NX, 128), F32),

time: 84.2 us -> 76.1 us (0.904)
  Pallas kernels: 82.1 us -> 74.1 us
    pallas_call x1, Pallas kernels: 82.1 us -> 74.1 us  [per_device(): pl.pallas_call(kernel, out_shape=jax.ShapeDtypeStruct((3, ROWS), F32), in...]
where the time goes in v3:
time: 76.1 us; the launch traced here: 76 us
  Pallas kernels  74.1 us (97%)
  other arithmetic  1.29 us (2%)
    pallas_call x1, Pallas kernels, per_device(): pl.pallas_call(kernel, out_shape=jax.ShapeDtypeStruct((3, ROWS), F32), in...  74.1 us

profile of v3, /device:TPU:2, one launch (start us, length us, event | category | flops | bytes accessed | tf_op | source)
XLA Modules:
  0.0 76.0 jit_solution(13934968118141233139)
XLA Ops:
  0.6 0.0 copy-start
  0.6 74.1 %shard_map.85 = f32[3,32]{1,0:T(4,128)} custom-call(bf16[2,16,512]{2,1,0:T(8,128)(2,1)} %bitcast.11, bf16[32,4096]{1,0:T(8,128)(2,1)} %train_in.1, bf16[592,4096]{1,0:T(8,128)(2,1)} %bitcast.10, s32[1,32]{1,0:T(1,128)} %bitcast.12, s32[1,32]{1,0:T(1,128)} %bitcast.13), custom_call_target="tpu_custom_call" | custom-call | flops 14227079168 | bytes 4849664 | tf_op jit(solution)/shard_map/pallas_call | solution.py:586
  74.7 0.0 copy-done
  74.7 1.3 %bitcast_multiply_fusion = (f32[32]{0:T(128)}, f32[32]{0:T(128)}, f32[32]{0:T(128)}) fusion(f32[3,32]{1,0:T(4,128)} %shard_map.85, s32[32]{0:T(128)S(1)} %copy-done), kind=kLoop, calls=%fused_computation | loop fusion | flops 128 | bytes 896 | tf_op jit(solution)/shard_map/mul | solution.py:621
Async XLA Ops:
  0.6 74.1 %copy-start = (s32[32]{0:T(128)S(1)}, s32[32]{0:T(128)}, u32[]{:S(2)}) copy-start(s32[32]{0:T(128)} %param.10) | copy-start | bytes 388

commit v4 on v3

--- a/solution.py
+++ b/solution.py
@@ -386,9 +386,11 @@
             need(("ms", 0))
             fill_onehot()
         elif task == "TS":
-            lax.fori_loop(0, NX, train_stats, 0)
+            for xx in range(NX):
+                train_stats(xx, 0)
         elif task == "RS":
-            lax.fori_loop(0, NX, roll_stats, 0)
+            for xx in range(NX):
+                roll_stats(xx, 0)
 
     def fill_onehot():
         place = lax.broadcasted_iota(jnp.int32, (TOK, GROUP), 0)
@@ -433,6 +435,8 @@
         return jnp.sum(jnp.where(diagonal, values, 0), axis=1, keepdims=True)
 
     def rows_of(xx):
+        if isinstance(xx, int):
+            return pl.ds(xx * GROUP, GROUP)
         return pl.ds(pl.multiple_of(xx * GROUP, GROUP), GROUP)
 
     tiles = [pl.ds(128 * j, 128) for j in range(WIDE // 128)]
@@ -529,7 +533,7 @@
     finish(0, column_r)
 
     def compare(xx, carry):
-        rows = pl.ds(pl.multiple_of(xx * GROUP, GROUP), GROUP)
+        rows = rows_of(xx)
         scale_r = jnp.exp(stat_r[xx, 0:1, :] - fin[0, 0, pl.ds(xx, 1), :]) / fin[0, 1, pl.ds(xx, 1), :]
         scale_t = jnp.exp(stat_t[xx, 0:1, :] - fin[1, 0, pl.ds(xx, 1), :]) / fin[1, 1, pl.ds(xx, 1), :]
         scale_r, scale_t = to_column(scale_r), to_column(scale_t)
@@ -550,7 +554,8 @@
                 one = one + jnp.where(part == k, pltpu.roll(values[k], ((k - zq) % 4) * ROWS, 1), 0.0)
             out2[xx, zq] = one
         return carry
-    lax.fori_loop(0, NX, compare, 0)
+    for xx in range(NX):
+        compare(xx, 0)
 
     a3[0] = out2[x, zh]
 

time: 76.1 us -> 74.1 us (0.974)
  Pallas kernels: 74.1 us -> 72 us
    pallas_call x1, Pallas kernels: 74.1 us -> 72 us  [per_device(): pl.pallas_call(kernel, out_shape=jax.ShapeDtypeStruct((3, ROWS), F32), in...]
where the time goes in v4:
time: 74.1 us; the launch traced here: 74 us
  Pallas kernels  72 us (97%)
  other arithmetic  1.29 us (2%)
    pallas_call x1, Pallas kernels, per_device(): pl.pallas_call(kernel, out_shape=jax.ShapeDtypeStruct((3, ROWS), F32), in...  72 us

profile of v4, /device:TPU:2, one launch (start us, length us, event | category | flops | bytes accessed | tf_op | source)
XLA Modules:
  0.0 74.0 jit_solution(8422819782226725203)
XLA Ops:
  0.6 0.0 copy-start
  0.6 72.0 %shard_map.85 = f32[3,32]{1,0:T(4,128)} custom-call(bf16[2,16,512]{2,1,0:T(8,128)(2,1)} %bitcast.11, bf16[32,4096]{1,0:T(8,128)(2,1)} %train_in.1, bf16[592,4096]{1,0:T(8,128)(2,1)} %bitcast.10, s32[1,32]{1,0:T(1,128)} %bitcast.12, s32[1,32]{1,0:T(1,128)} %bitcast.13), custom_call_target="tpu_custom_call" | custom-call | flops 14227079168 | bytes 4849664 | tf_op jit(solution)/shard_map/pallas_call | solution.py:591
  72.7 0.0 copy-done
  72.7 1.3 %bitcast_multiply_fusion = (f32[32]{0:T(128)}, f32[32]{0:T(128)}, f32[32]{0:T(128)}) fusion(f32[3,32]{1,0:T(4,128)} %shard_map.85, s32[32]{0:T(128)S(1)} %copy-done), kind=kLoop, calls=%fused_computation | loop fusion | flops 128 | bytes 896 | tf_op jit(solution)/shard_map/mul | solution.py:626
Async XLA Ops:
  0.6 72.0 %copy-start = (s32[32]{0:T(128)S(1)}, s32[32]{0:T(128)}, u32[]{:S(2)}) copy-start(s32[32]{0:T(128)} %param.10) | copy-start | bytes 388

commit v5 on v4

--- a/solution.py
+++ b/solution.py
@@ -530,18 +530,21 @@
     lax.fori_loop(0, NX, roll_picks, 0)
     column_r = column_z(0, plane_r)
     finish(1, column_t)
+    for xx in range(NX):
+        scale_t = to_column(jnp.exp(stat_t[xx, 0:1, :] - fin[1, 0, xx:xx + 1, :]) / fin[1, 1, xx:xx + 1, :])
+        for tile in tiles:
+            et[rows_of(xx), tile] = et[rows_of(xx), tile] * scale_t
     finish(0, column_r)
 
     def compare(xx, carry):
         rows = rows_of(xx)
         scale_r = jnp.exp(stat_r[xx, 0:1, :] - fin[0, 0, pl.ds(xx, 1), :]) / fin[0, 1, pl.ds(xx, 1), :]
-        scale_t = jnp.exp(stat_t[xx, 0:1, :] - fin[1, 0, pl.ds(xx, 1), :]) / fin[1, 1, pl.ds(xx, 1), :]
-        scale_r, scale_t = to_column(scale_r), to_column(scale_t)
+        scale_r = to_column(scale_r)
         shared = jnp.zeros((GROUP, 128), F32)
         squares = jnp.zeros((GROUP, 128), F32)
         for tile in tiles:
             p = er[rows, tile] * scale_r
-            q = et[rows, tile] * scale_t
+            q = et[rows, tile]
             shared = shared + jnp.minimum(p, q)
             squares = squares + (q - p) * (q - p)
         shared = to_row(jnp.sum(shared, axis=1, keepdims=True))

time: 74.1 us -> 73.9 us (level)
  no operation moved by 1% of the time
where the time goes in v5:
time: 73.9 us; the launch traced here: 73.8 us
  Pallas kernels  71.9 us (97%)
  other arithmetic  1.29 us (2%)
    pallas_call x1, Pallas kernels, per_device(): pl.pallas_call(kernel, out_shape=jax.ShapeDtypeStruct((3, ROWS), F32), in...  71.9 us

profile of v5, /device:TPU:2, one launch (start us, length us, event | category | flops | bytes accessed | tf_op | source)
XLA Modules:
  0.0 73.8 jit_solution(10500772873890783531)
XLA Ops:
  0.6 0.0 copy-start
  0.6 71.9 %shard_map.85 = f32[3,32]{1,0:T(4,128)} custom-call(bf16[2,16,512]{2,1,0:T(8,128)(2,1)} %bitcast.11, bf16[32,4096]{1,0:T(8,128)(2,1)} %train_in.1, bf16[592,4096]{1,0:T(8,128)(2,1)} %bitcast.10, s32[1,32]{1,0:T(1,128)} %bitcast.12, s32[1,32]{1,0:T(1,128)} %bitcast.13), custom_call_target="tpu_custom_call" | custom-call | flops 14227079168 | bytes 4849664 | tf_op jit(solution)/shard_map/pallas_call | solution.py:594
  72.5 0.0 copy-done
  72.5 1.3 %bitcast_multiply_fusion = (f32[32]{0:T(128)}, f32[32]{0:T(128)}, f32[32]{0:T(128)}) fusion(f32[3,32]{1,0:T(4,128)} %shard_map.85, s32[32]{0:T(128)S(1)} %copy-done), kind=kLoop, calls=%fused_computation | loop fusion | flops 128 | bytes 896 | tf_op jit(solution)/shard_map/mul | solution.py:629
Async XLA Ops:
  0.6 71.9 %copy-start = (s32[32]{0:T(128)S(1)}, s32[32]{0:T(128)}, u32[]{:S(2)}) copy-start(s32[32]{0:T(128)} %param.10) | copy-start | bytes 388
